TPU v7x, 32 devices: a whole 2x2x4 slice. The times are simulated.
32 devices in a mesh: seq: 8 (over z, x), tp: 4 (over y, core).
Axes of the slice: x: 2, y: 2, z: 4, core: 2. Of those that a mesh axis runs over, the one named last changes fastest.
Arguments:
- streams: bfloat16 [3, 4096, 2048], P(None, 'seq', 'tp'), may hold values from -6 to 6
- short_taps: float32 [3, 3, 2048], P(None, None, 'tp'), may hold values from -3 to 3
- filter_taps: float32 [4096, 2048], P('seq', 'tp'), may hold values from -0.09375 to 0.09375
- skip_gain: float32 [2048], P('tp'), may hold values from -4 to 4
- w_out: bfloat16 [2048, 4096], P('tp'), may hold values from -0.1875 to 0.1875
- cotangent: bfloat16 [4096, 4096], P('seq'), may hold values from -6 to 6
Outputs:
- mixed: bfloat16 [4096, 4096], P('seq', 'tp')
- stream_grads: bfloat16 [3, 4096, 2048], P(None, 'seq', 'tp')
All inputs are finite; a program needn't handle non-finite values.
Results may differ from a plain program's by a relative error of at most 0.005.
Values may be sent and summed in bfloat16 or wider, within the bound.
A program may use at most 128 MiB of HBM per device.

v0:
```python
import math

import jax
import jax.numpy as jnp
from jax import lax
from jax.sharding import PartitionSpec as P

full_turn = 2.0 * math.pi


def passed_along(x, axis, by):
    devices = lax.axis_size(axis)
    pairs = [(i, i + by) for i in range(devices) if 0 <= i + by < devices]
    return lax.ppermute(x, axis, pairs)


def angle_table(rows, cols, period):
    row_ids = jnp.arange(rows, dtype=jnp.int32)[:, None]
    col_ids = jnp.arange(cols, dtype=jnp.int32)[None, :]
    angles = (row_ids * col_ids % period).astype(jnp.float32) * (full_turn / period)
    return (jnp.cos(angles), jnp.sin(angles))


def lane_forward(lanes, total):
    count = lanes.shape[2]
    cosine, sine = angle_table(2 * count, count, 2 * count)
    table = jnp.stack([cosine, -sine])
    section = jnp.einsum("rkm,bmic->rbcki", table, lanes[0], precision=lax.Precision.HIGHEST)
    twist_cos, twist_sin = angle_table(2 * count, lanes.shape[3], total)
    real_part = section[0] * twist_cos + section[1] * twist_sin
    imag_part = section[1] * twist_cos - section[0] * twist_sin
    return jnp.stack([real_part, imag_part])


def lane_block(spectral, sign):
    length = spectral.shape[4]
    cosine, sine = angle_table(length, length, length)
    table = jnp.stack([jnp.stack([cosine, sign * sine]), jnp.stack([-sign * sine, cosine])])
    return jnp.einsum("rqji,qbcki->rbckj", table, spectral, precision=lax.Precision.HIGHEST)


def lane_inverse(spectral, total):
    count = spectral.shape[3] // 2
    twist_cos, twist_sin = angle_table(2 * count, spectral.shape[4], total)
    real_part = spectral[0] * twist_cos - spectral[1] * twist_sin
    imag_part = spectral[0] * twist_sin + spectral[1] * twist_cos
    cosine, sine = angle_table(count, 2 * count, 2 * count)
    table = jnp.stack([cosine, -sine]) * (1.0 / total)
    result = jnp.einsum(
        "rmk,rbcki->bmic", table, jnp.stack([real_part, imag_part]), precision=lax.Precision.HIGHEST
    )
    return result[None]


def spectrum(signal_block):
    devices = lax.axis_size("seq")
    length = signal_block.shape[3]
    total = 2 * length * devices
    lanes = lax.all_to_all(signal_block, "seq", split_axis=4, concat_axis=2, tiled=True)
    return lane_block(lane_forward(lanes, total), 1.0)


def back_to_signal(spectral, length):
    devices = lax.axis_size("seq")
    total = 2 * length * devices
    lanes = lane_inverse(lane_block(spectral, -1.0), total)
    restored = lax.all_to_all(lanes, "seq", split_axis=2, concat_axis=4, tiled=True)
    return restored[0, 0, 0]


def on_device(streams, short_taps, filter_taps, skip_gain, w_out, cotangent):
    length = streams.shape[1]
    previous = passed_along(streams[:, -2:, :], "seq", 1)
    extended = jnp.concatenate([previous, streams], axis=1).astype(jnp.float32)
    convolved = (
        short_taps[:, 0, None, :] * extended[:, 2:]
        + short_taps[:, 1, None, :] * extended[:, 1:-1]
        + short_taps[:, 2, None, :] * extended[:, :-2]
    )
    conv_q = convolved[0]
    conv_k = convolved[1]
    conv_v = convolved[2]
    source = conv_k * conv_v
    both_spectra = spectrum(jnp.stack([source, filter_taps])[None, :, None])
    data_real = both_spectra[0, 0]
    data_imag = both_spectra[1, 0]
    kernel_real = both_spectra[0, 1]
    kernel_imag = both_spectra[1, 1]
    product = jnp.stack(
        [
            data_real * kernel_real - data_imag * kernel_imag,
            data_real * kernel_imag + data_imag * kernel_real,
        ]
    )[:, None]
    mixer_state = back_to_signal(product, length) + skip_gain * source
    gated = (conv_q * mixer_state).astype(jnp.bfloat16)
    terms = jnp.dot(gated, w_out, preferred_element_type=jnp.float32)
    mixed = lax.psum_scatter(terms, "tp", scatter_dimension=1, tiled=True).astype(jnp.bfloat16)
    grad_gated = lax.dot_general(
        cotangent, w_out, (((1,), (1,)), ((), ())), preferred_element_type=jnp.float32
    )
    grad_q = grad_gated * mixer_state
    grad_state = grad_gated * conv_q
    grad_spectrum = spectrum(grad_state[None, None, None])
    grad_real = grad_spectrum[0, 0]
    grad_imag = grad_spectrum[1, 0]
    adjoint = jnp.stack(
        [
            grad_real * kernel_real + grad_imag * kernel_imag,
            grad_imag * kernel_real - grad_real * kernel_imag,
        ]
    )[:, None]
    grad_source = back_to_signal(adjoint, length) + skip_gain * grad_state
    gradients = jnp.stack([grad_q, grad_source * conv_v, grad_source * conv_k])
    following = passed_along(gradients[:, :2, :], "seq", -1)
    grad_ext = jnp.concatenate([gradients, following], axis=1)
    stream_grads = (
        short_taps[:, 0, None, :] * grad_ext[:, :-2]
        + short_taps[:, 1, None, :] * grad_ext[:, 1:-1]
        + short_taps[:, 2, None, :] * grad_ext[:, 2:]
    )
    return (mixed, stream_grads.astype(jnp.bfloat16))


def solution(mesh):
    return jax.shard_map(
        on_device,
        mesh=mesh,
        in_specs=(
            P(None, "seq", "tp"),
            P(None, None, "tp"),
            P("seq", "tp"),
            P("tp"),
            P("tp", None),
            P("seq", None),
        ),
        out_specs=(P("seq", "tp"), P(None, "seq", "tp")),
        check_vma=False,
    )
```

profile of v0, /device:TPU:0, one launch (start us, length us, event | category | flops | bytes accessed | tf_op | source)
XLA Modules:
  0.0 350.8 jit_solution(18106328003262360629)
XLA Ops:
  7.2 0.8 slice.93
  7.9 4.8 %collective-permute-start = (bf16[3,2,512]{2,1,0:T(2,128)(2,1)S(1)}, bf16[3,2,512]{2,1,0:T(2,128)(2,1)S(1)}, u32[]{:S(2)}, u32[]{:S(2)}) collective-permute-start(bf16[3,2,512]{2,1,0:T(2,128)(2,1)S(1)} %slice.93), channel_id=1, source_target_pairs={{0,4},{4,8},{8,12},{12,16},{16,20},{20,24},{24,28},{1,5},{5,9},{9,... | collective-permute-start | bytes 18440 | tf_op jit(solution)/shard_map/ppermute | solution.py:14
  12.8 0.9 fusion.108
  13.7 5.9 %fusion.109 = f32[512,512]{1,0:T(8,128)S(1)} fusion(bf16[512,4096]{1,0:T(8,128)(2,1)} %param.11, bf16[512,4096]{1,0:T(8,128)(2,1)} %param.10), kind=kOutput, calls=%fused_computation.164 | convolution fusion | flops 2147483648 | bytes 9437184 | tf_op jit(solution)/shard_map/dot_general | solution.py:99
  19.6 0.5 maximum_convert_fusion
  20.1 0.9 fusion.24
  21.1 1.2 fusion.67
  22.2 3.6 %copy.51 = f32[1,1,1,512,512]{3,2,1,0,4:T(1,128)} copy(f32[1,1,1,512,512]{4,3,2,1,0:T(8,128)} %fusion.67) | data formatting | bytes 2097152 | tf_op jit(solution)/shard_map/broadcast_in_dim | solution.py:104
  25.8 4.9 %all-to-all-start.2 = ((f32[1,1,1,512,512]{3,2,1,0,4:T(1,128)}), f32[1,1,1,512,512]{3,2,1,0,4:T(1,128)}, u32[]{:S(2)}, u32[]{:S(2)}) async-start(f32[1,1,1,512,512]{3,2,1,0,4:T(1,128)} %copy.51), calls=%async_computation.3 | async-start | bytes 2097152 | tf_op jit(solution)/shard_map/all_to_all | solution.py:59
  30.9 1.0 copy-done.12
  31.9 1.5 maximum_bitcast_fusion.21
  33.4 4.1 %copy.40 = f32[1,2,1,512,512]{3,1,2,0,4:T(2,128)} copy(f32[1,2,1,512,512]{4,3,1,2,0:T(8,128)} %maximum_bitcast_fusion.21) | data formatting | bytes 4194304 | tf_op jit(solution)/shard_map/broadcast_in_dim | solution.py:84
  37.6 18.8 %all-to-all-done.2 = f32[1,1,1,512,512]{3,2,1,0,4:T(1,128)} async-done(((f32[1,1,1,512,512]{3,2,1,0,4:T(1,128)}), f32[1,1,1,512,512]{3,2,1,0,4:T(1,128)}, u32[]{:S(2)}, u32[]{:S(2)}) %all-to-all-start.2) | async-done | bytes 1048608 | tf_op jit(solution)/shard_map/all_to_all | solution.py:59
  56.4 4.5 %all-to-all-start = ((f32[1,2,1,512,512]{3,1,2,0,4:T(2,128)}), f32[1,2,1,512,512]{3,1,2,0,4:T(2,128)}, u32[]{:S(2)}, u32[]{:S(2)}) async-start(f32[1,2,1,512,512]{3,1,2,0,4:T(2,128)} %copy.40), calls=%async_computation | async-start | bytes 4194304 | tf_op jit(solution)/shard_map/all_to_all | solution.py:59
  61.2 3.8 %fusion.66 = f32[1,512,512]{2,1,0:T(8,128)S(1)} fusion(), kind=kLoop, calls=%fused_computation.108 | loop fusion | flops 3670016 | bytes 1048576 | tf_op jit(solution)/shard_map/cos | solution.py:21
  65.0 3.9 %broadcast_multiply_fusion = (f32[1,512,512]{2,1,0:T(8,128)S(1)}, f32[1,512,512]{2,1,0:T(8,128)S(1)}) fusion(), kind=kLoop, calls=%fused_computation.106 | loop fusion | flops 3932160 | bytes 2097152 | tf_op jit(solution)/shard_map/mul | solution.py:38
  68.9 3.2 fusion.37
  72.1 2.1 copy.84
  74.1 4.3 %convolution_bitcast_fusion.1 = f32[2,1,64,16,512]{4,3,0,2,1:T(8,128)S(1)} fusion(f32[1,1,1,512,8,64]{3,5,4,2,1,0:T(8,128)S(1)} %bitcast.252, f32[1,16,8]{1,2,0:T(8,128)S(1)} %get-tuple-element.34, f32[1,16,8]{1,2,0:T(8,128)S(1)} %get-tuple-element.35), kind=kOutput, calls=%fused_computation.49 | convolution fusion | flops 100663552 | bytes 5243904 | tf_op jit(solution)/shard_map/rkm,bmic->rbcki/dot_general | solution.py:28
  78.4 1.0 multiply_add_fusion.2
  79.5 15.2 %fusion.32 = f32[2,1,64,16,512]{4,3,2,1,0:T(8,128)} fusion(f32[1,2,512,512]{3,2,1,0:T(8,128)S(1)} %get-tuple-element.24, f32[1,2,512,512]{3,2,1,0:T(8,128)S(1)} %get-tuple-element.19, f32[1,1,64,16,512]{4,3,0,2,1:T(8,128)S(1)} %get-tuple-element.14, f32[1,1,64,16,512]{4,3,0,2,1:T(8,128)S(1)} %get-tuple-element.13), kind=kOutput, calls=%fused_computation.48 | convolution fusion | flops 12886999040 | bytes 12582912 | tf_op jit(solution)/shard_map/rqji,qbcki->rbckj/dot_general | solution.py:39
  94.7 13.8 %all-to-all-done = f32[1,2,1,512,512]{3,1,2,0,4:T(2,128)} async-done(((f32[1,2,1,512,512]{3,1,2,0,4:T(2,128)}), f32[1,2,1,512,512]{3,1,2,0,4:T(2,128)}, u32[]{:S(2)}, u32[]{:S(2)}) %all-to-all-start) | async-done | bytes 2097184 | tf_op jit(solution)/shard_map/all_to_all | solution.py:59
  108.4 9.7 %convolution_bitcast_fusion = f32[2,2,64,16,512]{4,3,0,2,1:T(8,128)S(1)} fusion(f32[1,2,1,512,8,64]{3,1,5,4,2,0:T(2,128)} %bitcast.3, f32[1,16,8]{1,2,0:T(8,128)S(1)} %get-tuple-element.34, f32[1,16,8]{1,2,0:T(8,128)S(1)} %get-tuple-element.35), kind=kOutput, calls=%fused_computation.28 | convolution fusion | flops 201326848 | bytes 10486784 | tf_op jit(solution)/shard_map/rkm,bmic->rbcki/dot_general | solution.py:28
  118.2 4.5 %multiply_add_fusion = (f32[1,2,64,16,512]{4,3,0,2,1:T(8,128)}, f32[1,2,64,16,512]{4,3,0,2,1:T(8,128)}) fusion(f32[2,2,64,16,512]{4,3,0,2,1:T(8,128)S(1)} %convolution_bitcast_fusion, f32[16,512]{1,0:T(8,128)S(1)} %get-tuple-element.36, f32[16,512]{1,0:T(8,128)S(1)} %get-tuple-element.37), kind=kLoop, calls=%fused_computation.27 | loop fusion | flops 6291456 | bytes 16842752 | tf_op jit(solution)/shard_map/add | solution.py:30
  122.7 30.4 %fusion.18 = f32[2,2,64,16,512]{4,3,0,2,1:T(8,128)S(1)} fusion(f32[1,2,512,512]{3,2,1,0:T(8,128)} %copy-done.10, f32[1,2,512,512]{3,2,1,0:T(8,128)S(1)} %copy-done.9, f32[1,2,64,16,512]{4,3,0,2,1:T(8,128)} %get-tuple-element.7, f32[1,2,64,16,512]{4,3,0,2,1:T(8,128)} %get-tuple-element.6), kind=kOutput, calls=%fused_computation.29 | convolution fusion | flops 25772949504 | bytes 20971520 | tf_op jit(solution)/shard_map/rqji,qbcki->rbckj/dot_general | solution.py:39
  153.1 2.4 fusion.41
  155.5 3.8 %fusion.47 = (f32[1,64,16,512]{3,2,1,0:T(8,128)}, f32[1,64,16,512]{3,2,1,0:T(8,128)S(1)}, f32[1,64,16,512]{3,2,1,0:T(8,128)}) fusion(f32[2,1,64,16,512]{4,3,2,1,0:T(8,128)S(1)} %copy-done, f32[2,2,64,16,512]{4,3,0,2,1:T(8,128)S(1)} %fusion.18), kind=kLoop, calls=%fused_computation.70 | loop fusion | flops 4718592 | bytes 18874368 | tf_op jit(solution)/shard_map/add | solution.py:109
  159.3 17.5 %fusion.29 = f32[2,1,64,16,512]{4,3,0,2,1:T(8,128)S(1)} fusion(f32[1,2,512,512]{3,2,1,0:T(8,128)} %get-tuple-element.20, f32[1,2,512,512]{3,2,1,0:T(8,128)} %get-tuple-element.23, f32[1,64,16,512]{3,2,1,0:T(8,128)} %fusion.41, f32[1,64,16,512]{3,2,1,0:T(8,128)} %get-tuple-element.8), kind=kOutput, calls=%fused_computation.47 | convolution fusion | flops 12886999040 | bytes 12582912 | tf_op jit(solution)/shard_map/rqji,qbcki->rbckj/dot_general | solution.py:39
  176.8 14.1 %fusion.26 = f32[2,1,64,16,512]{4,3,0,2,1:T(8,128)S(1)} fusion(f32[1,2,512,512]{3,2,1,0:T(8,128)S(1)} %copy-done.6, f32[1,2,512,512]{3,2,1,0:T(8,128)S(1)} %copy-done.7, f32[1,64,16,512]{3,2,1,0:T(8,128)S(1)} %copy-done.5, f32[1,64,16,512]{3,2,1,0:T(8,128)S(1)} %get-tuple-element.9), kind=kOutput, calls=%fused_computation.46 | convolution fusion | flops 12886999040 | bytes 12582912 | tf_op jit(solution)/shard_map/rqji,qbcki->rbckj/dot_general | solution.py:39
  190.9 3.5 %multiply_subtract_fusion.1 = (f32[1,1,64,16,512]{4,3,0,2,1:T(8,128)S(1)}, f32[1,1,64,16,512]{4,3,0,2,1:T(8,128)S(1)}, f32[1,1,64,16,512]{4,3,0,2,1:T(8,128)}, f32[1,1,64,16,512]{4,3,0,2,1:T(8,128)}) fusion(f32[2,1,64,16,512]{4,3,0,2,1:T(8,128)S(1)} %fusion.29, f32[16,512]{1,0:T(8,128)S(1)} %get-tuple-element.36, f32[16,512]{1,0:T(8,128)S(1)} %get-tuple-element.37, ...), kind=kLoop, calls=%fused_computation.73 | loop fusion | flops 6291456 | bytes 16842752 | tf_op jit(solution)/shard_map/sub | solution.py:45
  194.5 2.3 fusion.49
  196.8 1.6 copy.58
  198.4 4.2 %all-to-all-start.3 = ((f32[1,1,8,512,64]{3,4,1,0,2:T(8,128)}), f32[1,1,8,512,64]{3,4,1,0,2:T(8,128)}, u32[]{:S(2)}, u32[]{:S(2)}) async-start(f32[1,1,8,512,64]{3,4,1,0,2:T(8,128)} %copy.58), calls=%async_computation.4 | async-start | bytes 2097152 | tf_op jit(solution)/shard_map/all_to_all | solution.py:67
  202.6 4.0 %fusion.50 = f32[1,1,8,512,64]{3,2,4,1,0:T(8,128)S(1)} fusion(f32[1,1,64,16,512]{4,3,0,2,1:T(8,128)} %get-tuple-element.25, f32[1,1,64,16,512]{4,3,0,2,1:T(8,128)} %get-tuple-element.26, f32[1,8,16]{2,1,0:T(8,128)S(1)} %get-tuple-element.38, f32[1,8,16]{2,1,0:T(8,128)S(1)} %get-tuple-element.39), kind=kOutput, calls=%fused_computation.83 | convolution fusion | flops 101712384 | bytes 5243904 | tf_op jit(solution)/shard_map/rmk,rbcki->bmic/dot_general | solution.py:49
  206.6 1.6 copy.49
  208.2 20.0 %all-to-all-done.3 = f32[1,1,8,512,64]{3,4,1,0,2:T(8,128)} async-done(((f32[1,1,8,512,64]{3,4,1,0,2:T(8,128)}), f32[1,1,8,512,64]{3,4,1,0,2:T(8,128)}, u32[]{:S(2)}, u32[]{:S(2)}) %all-to-all-start.3) | async-done | bytes 1048608 | tf_op jit(solution)/shard_map/all_to_all | solution.py:67
  228.2 4.2 %all-to-all-start.1 = ((f32[1,1,8,512,64]{3,4,1,0,2:T(8,128)}), f32[1,1,8,512,64]{3,4,1,0,2:T(8,128)}, u32[]{:S(2)}, u32[]{:S(2)}) async-start(f32[1,1,8,512,64]{3,4,1,0,2:T(8,128)} %copy.49), calls=%async_computation.1 | async-start | bytes 2097152 | tf_op jit(solution)/shard_map/all_to_all | solution.py:67
  232.7 2.5 copy.59
  235.3 22.6 %all-to-all-done.1 = f32[1,1,8,512,64]{3,4,1,0,2:T(8,128)} async-done(((f32[1,1,8,512,64]{3,4,1,0,2:T(8,128)}), f32[1,1,8,512,64]{3,4,1,0,2:T(8,128)}, u32[]{:S(2)}, u32[]{:S(2)}) %all-to-all-start.1) | async-done | bytes 1048608 | tf_op jit(solution)/shard_map/all_to_all | solution.py:67
  257.9 2.5 copy.50
  260.4 4.2 %fusion.57 = (f32[1,512,512]{2,1,0:T(8,128)}, f32[512,512]{1,0:T(8,128)}, f32[1,512,512]{2,1,0:T(8,128)}, f32[512,512]{1,0:T(8,128)S(1)}) fusion(f32[3,512,512]{2,1,0:T(8,128)S(1)} %fusion.24, f32[512,512]{1,0:T(8,128)} %copy.59, f32[512,512]{1,0:T(8,128)} %copy-done.4, f32[512]{0:T(512)S(1)} %copy-done.13, f32[512,512]{1,0:T(8,128)} %copy.50), kind=kLoop, calls=%fused_computation.93 | loop fusion | flops 2097152 | bytes 10487808 | tf_op jit(solution)/shard_map/stack | solution.py:114
  264.6 5.7 %fusion.64 = f32[512,4096]{1,0:T(8,128)} fusion(bf16[512,4096]{1,0:T(8,128)(2,1)S(1)} %copy-done.3, f32[512,512]{1,0:T(8,128)S(1)} %get-tuple-element.18, f32[3,512,512]{2,1,0:T(8,128)S(1)} %fusion.24), kind=kOutput, calls=%fused_computation.105 | convolution fusion | flops 2148007936 | bytes 14680064 | tf_op jit(solution)/shard_map/dot_general | solution.py:97
  270.4 1.6 fusion.58
  272.5 1.3 collective-permute-start.1
  273.8 4.3 %collective-permute-done.1 = f32[3,2,512]{2,1,0:T(2,128)S(1)} collective-permute-done((f32[3,2,512]{2,1,0:T(2,128)S(1)}, f32[3,2,512]{2,1,0:T(2,128)S(1)}, u32[]{:S(2)}, u32[]{:S(2)}) %collective-permute-start.1) | collective-permute-done | bytes 12320 | tf_op jit(solution)/shard_map/ppermute | solution.py:14
  278.5 2.2 fusion.22
  280.7 60.3 %reduce-scatter.2.cloned.1.call-done = f32[512,1024]{1,0:T(8,128)} async-done(((f32[512,4096]{1,0:T(8,128)}), f32[512,1024]{1,0:T(8,128)}) %reduce-scatter.2.cloned.1.call-update) | async-done | bytes 2097168 | tf_op jit(solution)/shard_map/reduce_scatter | solution.py:98
  341.0 2.7 convert_element_type.127
  (39 shorter events, 1.8 us)
Async XLA Ops:
  7.9 11.7 %collective-permute-start = (bf16[3,2,512]{2,1,0:T(2,128)(2,1)S(1)}, bf16[3,2,512]{2,1,0:T(2,128)(2,1)S(1)}, u32[]{:S(2)}, u32[]{:S(2)}) collective-permute-start(bf16[3,2,512]{2,1,0:T(2,128)(2,1)S(1)} %slice.93), channel_id=1, source_target_pairs={{0,4},{4,8},{8,12},{12,16},{16,20},{20,24},{24,28},{1,5},{5,9},{9,... | collective-permute-start | bytes 18440 | tf_op jit(solution)/shard_map/ppermute | solution.py:14
  13.6 6.0 %copy-start.11 = (bf16[3,512,512]{2,1,0:T(8,128)(2,1)S(1)}, bf16[3,512,512]{2,1,0:T(8,128)(2,1)}, u32[]{:S(2)}) copy-start(bf16[3,512,512]{2,1,0:T(8,128)(2,1)} %param.6) | copy-start | bytes 4718596
  19.6 1.5 copy-start.4
  25.8 30.6 %all-to-all-start.2 = ((f32[1,1,1,512,512]{3,2,1,0,4:T(1,128)}), f32[1,1,1,512,512]{3,2,1,0,4:T(1,128)}, u32[]{:S(2)}, u32[]{:S(2)}) async-start(f32[1,1,1,512,512]{3,2,1,0,4:T(1,128)} %copy.51), calls=%async_computation.3 | async-start | bytes 2097152 | tf_op jit(solution)/shard_map/all_to_all | solution.py:59
  30.7 1.2 copy-start.12
  56.4 52.0 %all-to-all-start = ((f32[1,2,1,512,512]{3,1,2,0,4:T(2,128)}), f32[1,2,1,512,512]{3,1,2,0,4:T(2,128)}, u32[]{:S(2)}, u32[]{:S(2)}) async-start(f32[1,2,1,512,512]{3,1,2,0,4:T(2,128)} %copy.40), calls=%async_computation | async-start | bytes 4194304 | tf_op jit(solution)/shard_map/all_to_all | solution.py:59
  72.1 7.4 %copy-start.8 = (f32[1,2,512,512]{3,2,1,0:T(8,128)}, f32[1,2,512,512]{3,2,1,0:T(8,128)S(1)}, u32[]{:S(2)}) copy-start(f32[1,2,512,512]{3,2,1,0:T(8,128)S(1)} %get-tuple-element.19) | copy-start | bytes 6291460
  72.1 7.4 %copy-start.10 = (f32[1,2,512,512]{3,2,1,0:T(8,128)}, f32[1,2,512,512]{3,2,1,0:T(8,128)S(1)}, u32[]{:S(2)}) copy-start(f32[1,2,512,512]{3,2,1,0:T(8,128)S(1)} %get-tuple-element.24) | copy-start | bytes 6291460
  118.2 4.5 %copy-start.9 = (f32[1,2,512,512]{3,2,1,0:T(8,128)S(1)}, f32[1,2,512,512]{3,2,1,0:T(8,128)}, u32[]{:S(2)}) copy-start(f32[1,2,512,512]{3,2,1,0:T(8,128)} %copy-done.8) | copy-start | bytes 6291460
  122.7 30.4 %copy-start = (f32[2,1,64,16,512]{4,3,2,1,0:T(8,128)S(1)}, f32[2,1,64,16,512]{4,3,2,1,0:T(8,128)}, u32[]{:S(2)}) copy-start(f32[2,1,64,16,512]{4,3,2,1,0:T(8,128)} %fusion.32) | copy-start | bytes 12582916
  159.3 17.5 %copy-start.5 = (f32[1,64,16,512]{3,2,1,0:T(8,128)S(1)}, f32[1,64,16,512]{3,2,1,0:T(8,128)}, u32[]{:S(2)}) copy-start(f32[1,64,16,512]{3,2,1,0:T(8,128)} %get-tuple-element.10) | copy-start | bytes 6291460
  159.3 17.5 %copy-start.6 = (f32[1,2,512,512]{3,2,1,0:T(8,128)S(1)}, f32[1,2,512,512]{3,2,1,0:T(8,128)}, u32[]{:S(2)}) copy-start(f32[1,2,512,512]{3,2,1,0:T(8,128)} %get-tuple-element.20) | copy-start | bytes 6291460
  159.3 17.5 %copy-start.7 = (f32[1,2,512,512]{3,2,1,0:T(8,128)S(1)}, f32[1,2,512,512]{3,2,1,0:T(8,128)}, u32[]{:S(2)}) copy-start(f32[1,2,512,512]{3,2,1,0:T(8,128)} %get-tuple-element.23) | copy-start | bytes 6291460
  198.4 29.9 %all-to-all-start.3 = ((f32[1,1,8,512,64]{3,4,1,0,2:T(8,128)}), f32[1,1,8,512,64]{3,4,1,0,2:T(8,128)}, u32[]{:S(2)}, u32[]{:S(2)}) async-start(f32[1,1,8,512,64]{3,4,1,0,2:T(8,128)} %copy.58), calls=%async_computation.4 | async-start | bytes 2097152 | tf_op jit(solution)/shard_map/all_to_all | solution.py:67
  208.2 52.2 %copy-start.13 = (f32[512]{0:T(512)S(1)}, f32[512]{0:T(512)}, u32[]{:S(2)}) copy-start(f32[512]{0:T(512)} %param.9) | copy-start | bytes 6148
  228.2 29.7 %all-to-all-start.1 = ((f32[1,1,8,512,64]{3,4,1,0,2:T(8,128)}), f32[1,1,8,512,64]{3,4,1,0,2:T(8,128)}, u32[]{:S(2)}, u32[]{:S(2)}) async-start(f32[1,1,8,512,64]{3,4,1,0,2:T(8,128)} %copy.49), calls=%async_computation.1 | async-start | bytes 2097152 | tf_op jit(solution)/shard_map/all_to_all | solution.py:67
  232.5 108.5 %reduce-scatter.2.cloned.1.call-start = ((), (), s32[]{:S(2)}) async-start(), calls=%async_computation.5 | async-start | bytes 10485760 | tf_op jit(solution)/shard_map/reduce_scatter | solution.py:98
  260.4 4.2 %copy-start.3 = (bf16[512,4096]{1,0:T(8,128)(2,1)S(1)}, bf16[512,4096]{1,0:T(8,128)(2,1)}, u32[]{:S(2)}) copy-start(bf16[512,4096]{1,0:T(8,128)(2,1)} %param.10) | copy-start | bytes 12582916
  270.3 1.6 copy-start.1
  270.4 1.8 copy-start.2
  272.5 5.6 %collective-permute-start.1 = (f32[3,2,512]{2,1,0:T(2,128)S(1)}, f32[3,2,512]{2,1,0:T(2,128)S(1)}, u32[]{:S(2)}, u32[]{:S(2)}) collective-permute-start(f32[3,2,512]{2,1,0:T(2,128)S(1)} %slice.139), channel_id=1, source_target_pairs={{4,0},{8,4},{12,8},{16,12},{20,16},{24,20},{28,24},{5,1},{9,5},{13... | collective-permute-start | bytes 36872 | tf_op jit(solution)/shard_map/ppermute | solution.py:14
Sparse Core Ops, SparseCore 0:
  270.5 70.5 reduce-scatter.1
where the time goes:
time: 356 us; the launch traced here: 351 us
  waiting for transfers between devices  140 us (39%)
  matrix products  109 us (31%)
  other arithmetic  42 us (12%)
  starting transfers between devices  24.3 us (7%)
  local copies, waits for them, and re-layouts  21 us (6%)
  between operations  14.6 us (4%)
    dot_general x4, matrix products, lane_block(): jnp.einsum('rqji,qbcki->rbckj', table, spectral, precision=lax.Precision....  77.2 us
    reduce_scatter x1, waiting for transfers between devices, on_device(): lax.psum_scatter(terms, 'tp', scatter_dimension=1, tiled=True)  60.3 us
    all_to_all x2, waiting for transfers between devices, back_to_signal(): lax.all_to_all(lanes, 'seq', split_axis=2, concat_axis=4, tiled=True)  42.6 us
    all_to_all x2, waiting for transfers between devices, spectrum(): lax.all_to_all(signal_block, 'seq', split_axis=4, concat_axis=2, tiled=True)  32.6 us
    dot_general x2, matrix products, lane_forward(): jnp.einsum('rkm,bmic->rbcki', table, lanes[0], precision=lax.Precision.HI...  14 us
    all_to_all x2, starting transfers between devices, spectrum(): lax.all_to_all(signal_block, 'seq', split_axis=4, concat_axis=2, tiled=True)  9.41 us
    all_to_all x2, starting transfers between devices, back_to_signal(): lax.all_to_all(lanes, 'seq', split_axis=2, concat_axis=4, tiled=True)  8.48 us
  transfers between devices with their start and end apart: 7, of which 6 were waited for; matrix products, arithmetic and copies ran while one was open for 17% of the time, Pallas kernels for 0%

commit v1 on v0

v1 whole, which is shorter than its diff:
```python
import functools
import math

import jax
import jax.numpy as jnp
import ml_dtypes
import numpy as np
from jax import lax
from jax.experimental import pallas as pl
from jax.experimental.pallas import tpu as pltpu
from jax.sharding import PartitionSpec as P


def passed_along(x, axis, by):
    devices = lax.axis_size(axis)
    pairs = [(i, i + by) for i in range(devices) if 0 <= i + by < devices]
    return lax.ppermute(x, axis, pairs)


def dft_tables(length):
    ids = np.arange(length)
    angles = (np.outer(ids, ids) % length) * (2.0 * math.pi / length)
    cosine, sine = np.cos(angles), np.sin(angles)
    table = np.block([[cosine, -sine], [sine, cosine]]).astype(np.float32)
    high = table.astype(ml_dtypes.bfloat16)
    low = (table - high.astype(np.float32)).astype(ml_dtypes.bfloat16)
    return high, low


def twiddle_table(devices, length):
    angles = -2.0 * math.pi * np.outer(np.arange(devices) + 0.25, np.arange(length)) / (devices * length)
    return np.stack([np.cos(angles), np.sin(angles)]).astype(np.float32)


def across_weights(devices):
    angles = -2.0 * math.pi * np.outer(np.arange(devices) + 0.25, np.arange(devices)) / devices
    return np.cos(angles), np.sin(angles)


def split_store(high_ref, low_ref, rows, lanes, value):
    high = value.astype(jnp.bfloat16)
    high_ref[rows, lanes] = high
    low_ref[rows, lanes] = (value - high.astype(jnp.float32)).astype(jnp.bfloat16)


row_step = 16
lane_step = 128


def tiles_of(channels, length, body):
    per_row = length // lane_step

    @pl.loop(0, (channels // row_step) * per_row)
    def _(step):
        row = pl.multiple_of((step // per_row) * row_step, row_step)
        lane = pl.multiple_of((step % per_row) * lane_step, lane_step)
        body(row, lane)


def forward_across(x_ref, twiddle_ref, high_ref, low_ref):
    devices, channels, length = x_ref.shape
    real_w, imag_w = across_weights(devices)

    def body(row, lane):
        lanes = pl.ds(lane, lane_step)
        values = [x_ref[m, pl.ds(row, row_step), lanes].astype(jnp.float32) for m in range(devices)]
        for k in range(devices):
            real = values[0] * float(real_w[k, 0])
            imag = None
            for m in range(1, devices):
                real = real + values[m] * float(real_w[k, m])
                term = values[m] * float(imag_w[k, m])
                imag = term if imag is None else imag + term
            twiddle_real = twiddle_ref[0, pl.ds(k, 1), lanes]
            twiddle_imag = twiddle_ref[1, pl.ds(k, 1), lanes]
            rows = pl.ds(pl.multiple_of(k * channels + row, row_step), row_step)
            split_store(high_ref, low_ref, rows, lanes, real * twiddle_real - imag * twiddle_imag)
            upper = pl.ds(pl.multiple_of(length + lane, lane_step), lane_step)
            split_store(high_ref, low_ref, rows, upper, real * twiddle_imag + imag * twiddle_real)

    tiles_of(channels, length, body)


def transform(high_ref, low_ref, table_high_ref, table_low_ref, out_ref):
    width = out_ref.shape[1]
    part = 256

    @pl.loop(0, width // part)
    def _(step):
        lanes = pl.ds(pl.multiple_of(step * part, part), part)
        dot = functools.partial(jnp.dot, preferred_element_type=jnp.float32)
        out_ref[:, lanes] = (
            dot(high_ref[...], table_high_ref[:, lanes])
            + dot(low_ref[...], table_high_ref[:, lanes])
            + dot(high_ref[...], table_low_ref[:, lanes])
        )


def spectrum_kernel(x_ref, twiddle_ref, table_high_ref, table_low_ref, out_ref, high_ref, low_ref):
    forward_across(x_ref, twiddle_ref, high_ref, low_ref)
    transform(high_ref, low_ref, table_high_ref, table_low_ref, out_ref)


def filter_kernel(sign, x_ref, spectrum_ref, twiddle_ref, table_high_ref, table_low_ref, out_ref, high_ref, low_ref, full_ref):
    devices, channels, length = x_ref.shape
    forward_across(x_ref, twiddle_ref, high_ref, low_ref)
    transform(high_ref, low_ref, table_high_ref, table_low_ref, full_ref)
    real_w, imag_w = across_weights(devices)
    scale = 1.0 / (devices * length)

    def multiply(row, lane):
        rows = pl.ds(row, row_step)
        lanes = pl.ds(lane, lane_step)
        upper = pl.ds(pl.multiple_of(length + lane, lane_step), lane_step)
        data_real, data_imag = full_ref[rows, lanes], full_ref[rows, upper]
        taps_real, taps_imag = spectrum_ref[rows, lanes], spectrum_ref[rows, upper] * sign
        split_store(high_ref, low_ref, rows, lanes, data_real * taps_real - data_imag * taps_imag)
        split_store(high_ref, low_ref, rows, upper, -(data_real * taps_imag + data_imag * taps_real))

    tiles_of(devices * channels, length, multiply)
    transform(high_ref, low_ref, table_high_ref, table_low_ref, full_ref)

    def inverse(row, lane):
        lanes = pl.ds(lane, lane_step)
        upper = pl.ds(pl.multiple_of(length + lane, lane_step), lane_step)
        sums = [None] * devices
        for k in range(devices):
            rows = pl.ds(pl.multiple_of(k * channels + row, row_step), row_step)
            twiddle_real = twiddle_ref[0, pl.ds(k, 1), lanes]
            twiddle_imag = twiddle_ref[1, pl.ds(k, 1), lanes]
            real, imag = full_ref[rows, lanes], full_ref[rows, upper]
            turned_real = real * twiddle_real - imag * twiddle_imag
            turned_imag = real * twiddle_imag + imag * twiddle_real
            for m in range(devices):
                term = turned_real * float(scale * real_w[k, m])
                if m:
                    term = term - turned_imag * float(scale * imag_w[k, m])
                sums[m] = term if sums[m] is None else sums[m] + term
        for m in range(devices):
            out_ref[m, pl.ds(row, row_step), lanes] = sums[m].astype(jnp.bfloat16)

    tiles_of(channels, length, inverse)


def tables_for(devices, length):
    high, low = dft_tables(length)
    return jnp.asarray(twiddle_table(devices, length)), jnp.asarray(high), jnp.asarray(low)


def spectrum(x, tables):
    devices, channels, length = x.shape
    rows = devices * channels
    return pl.pallas_call(
        spectrum_kernel,
        out_shape=jax.ShapeDtypeStruct((rows, 2 * length), jnp.float32),
        scratch_shapes=[pltpu.VMEM((rows, 2 * length), jnp.bfloat16)] * 2,
        compiler_params=pltpu.CompilerParams(vmem_limit_bytes=40 << 20),
        cost_estimate=pl.CostEstimate(
            flops=6 * rows * (2 * length) ** 2, bytes_accessed=8 << 20, transcendentals=0
        ),
    )(x, *tables)


def filtered(x, taps_spectrum, tables, sign):
    devices, channels, length = x.shape
    rows = devices * channels
    return pl.pallas_call(
        functools.partial(filter_kernel, sign),
        out_shape=jax.ShapeDtypeStruct(x.shape, jnp.bfloat16),
        scratch_shapes=[pltpu.VMEM((rows, 2 * length), jnp.bfloat16)] * 2
        + [pltpu.VMEM((rows, 2 * length), jnp.float32)],
        compiler_params=pltpu.CompilerParams(vmem_limit_bytes=40 << 20),
        cost_estimate=pl.CostEstimate(
            flops=12 * rows * (2 * length) ** 2, bytes_accessed=8 << 20, transcendentals=0
        ),
    )(x, taps_spectrum, *tables)


def to_channels(x):
    devices = lax.axis_size("seq")
    turned = x.astype(jnp.bfloat16).T
    moved = lax.all_to_all(turned, "seq", split_axis=0, concat_axis=0, tiled=True)
    return moved.reshape(devices, x.shape[1] // devices, x.shape[0])


def to_positions(x):
    devices, channels, length = x.shape
    moved = lax.all_to_all(x.reshape(devices * channels, length), "seq", split_axis=0, concat_axis=0, tiled=True)
    return moved.T.astype(jnp.float32)


def on_device(streams, short_taps, filter_taps, skip_gain, w_out, cotangent):
    length = streams.shape[1]
    devices = lax.axis_size("seq")
    tables = tables_for(devices, length)
    taps_channels = to_channels(filter_taps)
    previous = passed_along(streams[:, -2:, :], "seq", 1)
    extended = jnp.concatenate([previous, streams], axis=1).astype(jnp.float32)
    convolved = (
        short_taps[:, 0, None, :] * extended[:, 2:]
        + short_taps[:, 1, None, :] * extended[:, 1:-1]
        + short_taps[:, 2, None, :] * extended[:, :-2]
    )
    conv_q = convolved[0]
    conv_k = convolved[1]
    conv_v = convolved[2]
    source = conv_k * conv_v
    grad_gated = lax.dot_general(
        cotangent, w_out, (((1,), (1,)), ((), ())), preferred_element_type=jnp.float32
    )
    grad_state = grad_gated * conv_q
    w_columns = lax.all_to_all(w_out, "tp", split_axis=1, concat_axis=0, tiled=True)
    taps_spectrum = spectrum(taps_channels, tables)
    mixer_state = to_positions(filtered(to_channels(source), taps_spectrum, tables, 1.0)) + skip_gain * source
    gated = (conv_q * mixer_state).astype(jnp.bfloat16)
    all_gated = lax.all_gather(gated, "tp", axis=1, tiled=True)
    mixed = jnp.dot(all_gated, w_columns, preferred_element_type=jnp.float32).astype(jnp.bfloat16)
    grad_q = grad_gated * mixer_state
    grad_source = to_positions(filtered(to_channels(grad_state), taps_spectrum, tables, -1.0)) + skip_gain * grad_state
    gradients = jnp.stack([grad_q, grad_source * conv_v, grad_source * conv_k])
    following = passed_along(gradients[:, :2, :], "seq", -1)
    grad_ext = jnp.concatenate([gradients, following], axis=1)
    stream_grads = (
        short_taps[:, 0, None, :] * grad_ext[:, :-2]
        + short_taps[:, 1, None, :] * grad_ext[:, 1:-1]
        + short_taps[:, 2, None, :] * grad_ext[:, 2:]
    )
    return (mixed, stream_grads.astype(jnp.bfloat16))


def solution(mesh):
    return jax.shard_map(
        on_device,
        mesh=mesh,
        in_specs=(
            P(None, "seq", "tp"),
            P(None, None, "tp"),
            P("seq", "tp"),
            P("tp"),
            P("tp", None),
            P("seq", None),
        ),
        out_specs=(P("seq", "tp"), P(None, "seq", "tp")),
        check_vma=False,
    )
```

time: 356 us -> 211 us (0.59); the launches traced: 351 us -> 210 us
  matrix products: 109 us -> 12 us
  waiting for transfers between devices: 140 us -> 66.4 us
  Pallas kernels: 0 us -> 34.9 us
  other arithmetic: 42 us -> 14.6 us
  local copies, waits for them, and re-layouts: 21 us -> 32.5 us
  starting transfers between devices: 24.3 us -> 35.4 us
    dot_general x9 -> x1, matrix products: 103 us -> 6.12 us  [on_device(): jnp.dot(all_gated, w_columns, preferred_element_type=jnp.float32)]
    reduce_scatter x1 -> x0, waiting for transfers between devices: 60.3 us -> none  [on_device(): lax.psum_scatter(terms, 'tp', scatter_dimension=1, tiled=True)]
    pallas_call x0 -> x3, Pallas kernels: none -> 34.9 us  [the longest x2 29.3 us: filtered(): pl.pallas_call(functools.partial(filter_kernel, sign), out_shape=jax.Shap...]
    unnamed x31 -> x37, local copies, waits for them, and re-layouts: 3.36 us -> 18.5 us
    all_to_all x4 -> x6, waiting for transfers between devices: 75.3 us -> 62.1 us  [the longest x1 39.4 us: on_device(): lax.all_to_all(w_out, 'tp', split_axis=1, concat_axis=0, tiled=True)]
    all_to_all x4 -> x6, starting transfers between devices: 17.9 us -> 29 us  [the longest x3 12.1 us: to_channels(): lax.all_to_all(turned, 'seq', split_axis=0, concat_axis=0, tiled=True)]
    broadcast_in_dim x4 -> x0, local copies, waits for them, and re-layouts: 10.9 us -> none  [the longest x1 4.15 us: on_device(): both_spectra = spectrum(jnp.stack([source, filter_taps])[None, :, None])]
    add x3 -> x0, other arithmetic: 9.32 us -> none  [the longest x2 5.51 us: lane_forward(): real_part = section[0] * twist_cos + section[1] * twist_sin]
  transfers between devices with their start and end apart: 7 -> 9, of which waited for: 6 -> 5; matrix products, arithmetic and copies ran while one was open for 17% -> 19% of each run, Pallas kernels for 0% -> 17%
where the time goes in v1:
time: 211 us; the launch traced here: 210 us
  waiting for transfers between devices  66.4 us (31%)
  starting transfers between devices  35.4 us (17%)
  Pallas kernels  34.9 us (17%)
  local copies, waits for them, and re-layouts  32.5 us (15%)
  other arithmetic  14.6 us (7%)
  between operations  14.3 us (7%)
  matrix products  12 us (6%)
    all_to_all x1, waiting for transfers between devices, on_device(): lax.all_to_all(w_out, 'tp', split_axis=1, concat_axis=0, tiled=True)  39.4 us
    pallas_call x2, Pallas kernels, filtered(): pl.pallas_call(functools.partial(filter_kernel, sign), out_shape=jax.Shap...  29.3 us
    unnamed x37, local copies, waits for them, and re-layouts  18.5 us
    all_to_all x3, waiting for transfers between devices, to_channels(): lax.all_to_all(turned, 'seq', split_axis=0, concat_axis=0, tiled=True)  17.2 us
    all_to_all x3, starting transfers between devices, to_channels(): lax.all_to_all(turned, 'seq', split_axis=0, concat_axis=0, tiled=True)  12.1 us
    all_to_all x2, starting transfers between devices, to_positions(): lax.all_to_all(x.reshape(devices * channels, length), 'seq', split_axis=0...  12 us
    another operation x3, other arithmetic, on_device(): gradients = jnp.stack([grad_q, grad_source * conv_v, grad_source * conv_k])  6.49 us
    all_to_all x1, local copies, waits for them, and re-layouts, on_device(): lax.all_to_all(w_out, 'tp', split_axis=1, concat_axis=0, tiled=True)  6.29 us
  transfers between devices with their start and end apart: 9, of which 5 were waited for; matrix products, arithmetic and copies ran while one was open for 19% of the time, Pallas kernels for 17%

profile of v1, /device:TPU:0, one launch (start us, length us, event | category | flops | bytes accessed | tf_op | source)
XLA Modules:
  0.0 210.2 jit_solution(6716522089550263902)
XLA Ops:
  7.2 0.8 slice.43
  7.9 4.8 %collective-permute-start = (bf16[3,2,512]{2,1,0:T(2,128)(2,1)S(1)}, bf16[3,2,512]{2,1,0:T(2,128)(2,1)S(1)}, u32[]{:S(2)}, u32[]{:S(2)}) collective-permute-start(bf16[3,2,512]{2,1,0:T(2,128)(2,1)S(1)} %slice.43), channel_id=1, source_target_pairs={{0,4},{4,8},{8,12},{12,16},{16,20},{20,24},{24,28},{1,5},{5,9},{9,... | collective-permute-start | bytes 18440 | tf_op jit(solution)/shard_map/ppermute | solution.py:17
  12.8 1.3 convert_bitcast_fusion.1
  14.1 1.0 copy.22
  15.1 4.9 %all-to-all-start.1 = ((bf16[8,64,512]{2,1,0:T(8,128)(2,1)}), bf16[8,64,512]{2,1,0:T(8,128)(2,1)S(1)}, u32[]{:S(2)}, u32[]{:S(2)}) async-start(bf16[8,64,512]{2,1,0:T(8,128)(2,1)} %bitcast.6), calls=%async_computation.1 | async-start | bytes 1048576 | tf_op jit(solution)/shard_map/all_to_all | solution.py:182
  20.0 5.9 %fusion.8 = f32[512,512]{1,0:T(8,128)S(1)} fusion(bf16[512,4096]{1,0:T(8,128)(2,1)} %param.14, bf16[512,4096]{1,0:T(8,128)(2,1)} %param.13), kind=kOutput, calls=%fused_computation.34 | convolution fusion | flops 2147483648 | bytes 9437184 | tf_op jit(solution)/shard_map/dot_general | solution.py:208
  26.0 0.5 maximum_convert_fusion
  26.5 0.9 fusion.3
  27.4 1.6 copy-done.8
  29.1 0.4 convert_bitcast_fusion
  29.5 1.0 copy.26
  30.5 3.7 %all-to-all-done.1.x_ref = bf16[8,64,512]{2,1,0:T(8,128)(2,1)S(1)} async-done(((bf16[8,64,512]{2,1,0:T(8,128)(2,1)}), bf16[8,64,512]{2,1,0:T(8,128)(2,1)S(1)}, u32[]{:S(2)}, u32[]{:S(2)}) %all-to-all-start.1) | async-done | bytes 524320 | tf_op jit(solution)/shard_map/all_to_all | solution.py:182
  34.2 3.6 %all-to-all-start.4 = ((bf16[8,64,512]{2,1,0:T(8,128)(2,1)}), bf16[8,64,512]{2,1,0:T(8,128)(2,1)S(1)}, u32[]{:S(2)}, u32[]{:S(2)}) async-start(bf16[8,64,512]{2,1,0:T(8,128)(2,1)} %bitcast.14), calls=%async_computation.4 | async-start | bytes 1048576 | tf_op jit(solution)/shard_map/all_to_all | solution.py:182
  37.8 1.0 copy.21
  38.8 13.5 %all-to-all-done.4.x_ref = bf16[8,64,512]{2,1,0:T(8,128)(2,1)S(1)} async-done(((bf16[8,64,512]{2,1,0:T(8,128)(2,1)}), bf16[8,64,512]{2,1,0:T(8,128)(2,1)S(1)}, u32[]{:S(2)}, u32[]{:S(2)}) %all-to-all-start.4) | async-done | bytes 524320 | tf_op jit(solution)/shard_map/all_to_all | solution.py:182
  52.3 3.6 %all-to-all-start = ((bf16[8,64,512]{2,1,0:T(8,128)(2,1)}), bf16[8,64,512]{2,1,0:T(8,128)(2,1)S(1)}, u32[]{:S(2)}, u32[]{:S(2)}) async-start(bf16[8,64,512]{2,1,0:T(8,128)(2,1)} %bitcast.4), calls=%async_computation | async-start | bytes 1048576 | tf_op jit(solution)/shard_map/all_to_all | solution.py:182
  56.0 1.6 copy-done
  57.6 1.6 copy-done.3
  59.1 5.6 %shard_map.104.spectrum_ref = f32[512,1024]{1,0:T(8,128)S(1)} custom-call(bf16[8,64,512]{2,1,0:T(8,128)(2,1)S(1)} %all-to-all-done.1.x_ref, f32[2,8,512]{2,1,0:T(8,128)S(1)} %copy-done.5, bf16[1024,1024]{1,0:T(8,128)(2,1)S(1)} %copy-done.3, bf16[1024,1024]{1,0:T(8,128)(2,1)S(1)} %copy-done), custom_call_target="tpu_custom_call" | custom-call | flops 3221225472 | bytes 8388608 | tf_op jit(solution)/shard_map/pallas_call | solution.py:153
  64.8 14.7 %shard_map.106 = bf16[8,64,512]{2,1,0:T(8,128)(2,1)} custom-call(bf16[8,64,512]{2,1,0:T(8,128)(2,1)S(1)} %all-to-all-done.4.x_ref, f32[512,1024]{1,0:T(8,128)S(1)} %shard_map.104.spectrum_ref, f32[2,8,512]{2,1,0:T(8,128)S(1)} %copy-done.5, bf16[1024,1024]{1,0:T(8,128)(2,1)S(1)} %copy-done.3, bf16[1024,1024]{1,0:T(8,128)(2,1)S(1)} %copy-done.1), custom_call_target="tpu_custom_call" | custom-call | flops 6442450944 | bytes 8388608 | tf_op jit(solution)/shard_map/pallas_call | solution.py:167
  79.5 1.4 copy-done.6
  80.9 6.0 %all-to-all-start.5 = ((bf16[8,64,512]{2,1,0:T(8,128)(2,1)}), bf16[8,64,512]{2,1,0:T(8,128)(2,1)S(1)}, u32[]{:S(2)}, u32[]{:S(2)}) async-start(bf16[8,64,512]{2,1,0:T(8,128)(2,1)} %shard_map.106), calls=%async_computation.5 | async-start | bytes 1048576 | tf_op jit(solution)/shard_map/all_to_all | solution.py:188
  86.9 1.6 copy-done.2
  88.5 1.6 copy-done.4
  90.0 1.6 copy-done.7
  91.6 14.6 %shard_map.105 = bf16[8,64,512]{2,1,0:T(8,128)(2,1)} custom-call(bf16[8,64,512]{2,1,0:T(8,128)(2,1)S(1)} %all-to-all-done.x_ref, f32[512,1024]{1,0:T(8,128)S(1)} %copy-done.7, f32[2,8,512]{2,1,0:T(8,128)S(1)} %copy-done.5, bf16[1024,1024]{1,0:T(8,128)(2,1)S(1)} %copy-done.4, bf16[1024,1024]{1,0:T(8,128)(2,1)S(1)} %copy-done.2), custom_call_target="tpu_custom_call" | custom-call | flops 6442450944 | bytes 8388608 | tf_op jit(solution)/shard_map/pallas_call | solution.py:167
  106.2 6.0 %all-to-all-start.2 = ((bf16[8,64,512]{2,1,0:T(8,128)(2,1)}), bf16[8,64,512]{2,1,0:T(8,128)(2,1)S(1)}, u32[]{:S(2)}, u32[]{:S(2)}) async-start(bf16[8,64,512]{2,1,0:T(8,128)(2,1)} %shard_map.105), calls=%async_computation.2 | async-start | bytes 1048576 | tf_op jit(solution)/shard_map/all_to_all | solution.py:188
  112.2 6.5 %copy.24 = bf16[512,4096]{0,1:T(8,128)(2,1)} copy(bf16[512,4096]{1,0:T(8,128)(2,1)} %param.13) | data formatting | bytes 8388608 | tf_op args[4]
  118.7 0.2 bitcast_convert_fusion
  118.8 1.4 copy.27
  120.2 5.6 %all-to-all-done.2 = bf16[8,64,512]{2,1,0:T(8,128)(2,1)S(1)} async-done(((bf16[8,64,512]{2,1,0:T(8,128)(2,1)}), bf16[8,64,512]{2,1,0:T(8,128)(2,1)S(1)}, u32[]{:S(2)}, u32[]{:S(2)}) %all-to-all-start.2) | async-done | bytes 524320 | tf_op jit(solution)/shard_map/all_to_all | solution.py:188
  125.8 0.8 copy-done.13
  126.6 4.9 %all-to-all-start.3 = ((bf16[512,4,1024]{0,2,1:T(8,128)(2,1)}), bf16[512,4,1024]{0,2,1:T(8,128)(2,1)}, u32[]{:S(2)}, u32[]{:S(2)}) async-start(bf16[512,4,1024]{0,2,1:T(8,128)(2,1)} %bitcast.79), calls=%async_computation.3 | async-start | bytes 8388608 | tf_op jit(solution)/shard_map/all_to_all | solution.py:212
  131.5 0.2 all-gather.2.cloned.1.call-start
  131.7 2.3 %bitcast_convert_fusion.1 = f32[512,512]{1,0:T(8,128)} fusion(bf16[8,64,512]{2,1,0:T(8,128)(2,1)} %copy-done.13), kind=kLoop, calls=%fused_computation.26 | loop fusion | flops 262144 | bytes 1572864 | tf_op jit(solution)/shard_map/convert_element_type | solution.py:189
  134.0 2.5 %copy.23 = f32[512,512]{0,1:T(8,128)} copy(f32[512,512]{1,0:T(8,128)} %bitcast_convert_fusion.1) | data formatting | bytes 2097152 | tf_op jit(solution)/shard_map/convert_element_type | solution.py:189
  136.6 4.6 %multiply_bitcast_fusion.2 = (f32[1,512,512]{2,1,0:T(8,128)}, bf16[512,512]{1,0:T(8,128)(2,1)}, f32[1,512,512]{2,1,0:T(8,128)}, f32[512,512]{1,0:T(8,128)}) fusion(f32[512,512]{1,0:T(8,128)} %copy-done.12, f32[512]{0:T(512)S(1)} %copy-done.16, f32[512,512]{0,1:T(8,128)} %copy.23, f32[3,512,512]{2,1,0:T(8,128)S(1)} %copy-done.9, f32[512,512]{0,1:T(8,128)} %copy.27), kind=kLoop, calls=%fused_computation.21 | loop fusion | flops 2621440 | bytes 9963520 | tf_op jit(solution)/shard_map/stack | solution.py:220
  141.2 0.0 all-gather.2.cloned.1.call-update
  141.2 1.6 multiply_bitcast_fusion
  142.8 0.2 copy-done.11
  143.0 0.3 pad_maximum_fusion.1
  143.4 1.3 collective-permute-start.1
  144.7 4.3 %collective-permute-done.1 = f32[3,2,512]{2,1,0:T(2,128)S(1)} collective-permute-done((f32[3,2,512]{2,1,0:T(2,128)S(1)}, f32[3,2,512]{2,1,0:T(2,128)S(1)}, u32[]{:S(2)}, u32[]{:S(2)}) %collective-permute-start.1) | collective-permute-done | bytes 12320 | tf_op jit(solution)/shard_map/ppermute | solution.py:17
  149.0 0.4 pad_maximum_fusion
  149.4 2.2 %fusion.1 = bf16[3,512,512]{2,1,0:T(8,128)(2,1)} fusion(f32[3,514,512]{2,1,0:T(8,128)S(1)} %pad_maximum_fusion, f32[3,512]{1,0:T(4,128)S(1)} %get-tuple-element.13, f32[3,512]{1,0:T(4,128)S(1)} %get-tuple-element.14, f32[3,512]{1,0:T(4,128)S(1)} %bitcast.82, f32[1,512,512]{2,1,0:T(8,128)S(1)} %multiply_bitcast_fusion, f32[1,512,512]{2,1,0:T(8,128)S(1)} %copy-done.11, ...), kind=kLoop, calls=%fused_computation.3 | loop fusion | flops 6291456 | bytes 11028480 | tf_op jit(solution)/shard_map/convert_element_type | solution.py:228
  151.6 39.4 %all-to-all-done.3 = bf16[512,4,1024]{0,2,1:T(8,128)(2,1)} async-done(((bf16[512,4,1024]{0,2,1:T(8,128)(2,1)}), bf16[512,4,1024]{0,2,1:T(8,128)(2,1)}, u32[]{:S(2)}, u32[]{:S(2)}) %all-to-all-start.3) | async-done | bytes 4194336 | tf_op jit(solution)/shard_map/all_to_all | solution.py:212
  190.9 6.3 %copy.25 = bf16[4,512,1024]{2,1,0:T(8,128)(2,1)} copy(bf16[4,512,1024]{1,2,0:T(8,128)(2,1)} %bitcast.10) | data formatting | bytes 8388608 | tf_op jit(solution)/shard_map/all_to_all | solution.py:212
  197.2 6.1 %convolution_convert_fusion = bf16[512,1024]{1,0:T(8,128)(2,1)} fusion(bf16[512,2048]{1,0:T(8,128)(2,1)} %all-gather.2.cloned.1.call-done, bf16[2048,1024]{1,0:T(8,128)(2,1)} %bitcast.80), kind=kOutput, calls=%fused_computation.13 | convolution fusion | flops 2148007936 | bytes 7340032 | tf_op jit(solution)/shard_map/dot_general | solution.py:217
  (33 shorter events, 0.1 us)
Async XLA Ops:
  7.2 12.8 %copy-start.15 = (f32[3,3,512]{2,1,0:T(4,128)S(1)}, f32[3,3,512]{2,1,0:T(4,128)}, u32[]{:S(2)}) copy-start(f32[3,3,512]{2,1,0:T(4,128)} %param.10) | copy-start | bytes 55300
  7.9 18.0 %collective-permute-start = (bf16[3,2,512]{2,1,0:T(2,128)(2,1)S(1)}, bf16[3,2,512]{2,1,0:T(2,128)(2,1)S(1)}, u32[]{:S(2)}, u32[]{:S(2)}) collective-permute-start(bf16[3,2,512]{2,1,0:T(2,128)(2,1)S(1)} %slice.43), channel_id=1, source_target_pairs={{0,4},{4,8},{8,12},{12,16},{16,20},{20,24},{24,28},{1,5},{5,9},{9,... | collective-permute-start | bytes 18440 | tf_op jit(solution)/shard_map/ppermute | solution.py:17
  15.1 19.1 %all-to-all-start.1 = ((bf16[8,64,512]{2,1,0:T(8,128)(2,1)}), bf16[8,64,512]{2,1,0:T(8,128)(2,1)S(1)}, u32[]{:S(2)}, u32[]{:S(2)}) async-start(bf16[8,64,512]{2,1,0:T(8,128)(2,1)} %bitcast.6), calls=%async_computation.1 | async-start | bytes 1048576 | tf_op jit(solution)/shard_map/all_to_all | solution.py:182
  20.0 6.0 %copy-start.14 = (bf16[3,512,512]{2,1,0:T(8,128)(2,1)S(1)}, bf16[3,512,512]{2,1,0:T(8,128)(2,1)}, u32[]{:S(2)}) copy-start(bf16[3,512,512]{2,1,0:T(8,128)(2,1)} %param.9) | copy-start | bytes 4718596
  25.9 1.5 copy-start.12
  27.4 1.6 copy-start.8
  29.5 26.5 %copy-start.5 = (f32[2,8,512]{2,1,0:T(8,128)S(1)}, f32[2,8,512]{2,1,0:T(8,128)}, u32[]{:S(2)}) copy-start(f32[2,8,512]{2,1,0:T(8,128)} %constant.6.clone.twiddle_ref) | copy-start | bytes 98308
  34.2 18.1 %all-to-all-start.4 = ((bf16[8,64,512]{2,1,0:T(8,128)(2,1)}), bf16[8,64,512]{2,1,0:T(8,128)(2,1)S(1)}, u32[]{:S(2)}, u32[]{:S(2)}) async-start(bf16[8,64,512]{2,1,0:T(8,128)(2,1)} %bitcast.14), calls=%async_computation.4 | async-start | bytes 1048576 | tf_op jit(solution)/shard_map/all_to_all | solution.py:182
  52.3 28.6 %all-to-all-start = ((bf16[8,64,512]{2,1,0:T(8,128)(2,1)}), bf16[8,64,512]{2,1,0:T(8,128)(2,1)S(1)}, u32[]{:S(2)}, u32[]{:S(2)}) async-start(bf16[8,64,512]{2,1,0:T(8,128)(2,1)} %bitcast.4), calls=%async_computation | async-start | bytes 1048576 | tf_op jit(solution)/shard_map/all_to_all | solution.py:182
  56.0 1.6 copy-start
  57.6 1.6 copy-start.3
  59.1 5.6 %copy-start.1 = (bf16[1024,1024]{1,0:T(8,128)(2,1)S(1)}, bf16[1024,1024]{1,0:T(8,128)(2,1)}, u32[]{:S(2)}) copy-start(bf16[1024,1024]{1,0:T(8,128)(2,1)} %constant.8.clone.table_low_ref) | copy-start | bytes 6291460
  79.5 1.4 copy-start.6
  80.9 25.3 %all-to-all-start.5 = ((bf16[8,64,512]{2,1,0:T(8,128)(2,1)}), bf16[8,64,512]{2,1,0:T(8,128)(2,1)S(1)}, u32[]{:S(2)}, u32[]{:S(2)}) async-start(bf16[8,64,512]{2,1,0:T(8,128)(2,1)} %shard_map.106), calls=%async_computation.5 | async-start | bytes 1048576 | tf_op jit(solution)/shard_map/all_to_all | solution.py:188
  86.9 1.6 copy-start.2
  88.5 1.6 copy-start.4
  90.0 1.6 copy-start.7
  106.2 19.5 %all-to-all-start.2 = ((bf16[8,64,512]{2,1,0:T(8,128)(2,1)}), bf16[8,64,512]{2,1,0:T(8,128)(2,1)S(1)}, u32[]{:S(2)}, u32[]{:S(2)}) async-start(bf16[8,64,512]{2,1,0:T(8,128)(2,1)} %shard_map.105), calls=%async_computation.2 | async-start | bytes 1048576 | tf_op jit(solution)/shard_map/all_to_all | solution.py:188
  125.7 0.8 copy-start.13
  126.6 64.4 %all-to-all-start.3 = ((bf16[512,4,1024]{0,2,1:T(8,128)(2,1)}), bf16[512,4,1024]{0,2,1:T(8,128)(2,1)}, u32[]{:S(2)}, u32[]{:S(2)}) async-start(bf16[512,4,1024]{0,2,1:T(8,128)(2,1)} %bitcast.79), calls=%async_computation.3 | async-start | bytes 8388608 | tf_op jit(solution)/shard_map/all_to_all | solution.py:212
  131.5 5.1 %copy-start.9 = (f32[3,512,512]{2,1,0:T(8,128)S(1)}, f32[3,512,512]{2,1,0:T(8,128)}, u32[]{:S(2)}) copy-start(f32[3,512,512]{2,1,0:T(8,128)} %copy-done.8) | copy-start | bytes 9437188
  131.5 5.1 %copy-start.16 = (f32[512]{0:T(512)S(1)}, f32[512]{0:T(512)}, u32[]{:S(2)}) copy-start(f32[512]{0:T(512)} %param.12) | copy-start | bytes 6148
  131.5 65.7 %all-gather.2.cloned.1.call-start = ((), (), s32[]{:S(2)}) async-start(), calls=%async_computation.6 | async-start | bytes 2621440 | tf_op jit(solution)/shard_map/all_gather | solution.py:216
  141.2 1.6 copy-start.10
  141.2 1.8 copy-start.11
  143.4 5.6 %collective-permute-start.1 = (f32[3,2,512]{2,1,0:T(2,128)S(1)}, f32[3,2,512]{2,1,0:T(2,128)S(1)}, u32[]{:S(2)}, u32[]{:S(2)}) collective-permute-start(f32[3,2,512]{2,1,0:T(2,128)S(1)} %slice.61), channel_id=1, source_target_pairs={{4,0},{8,4},{12,8},{16,12},{20,16},{24,20},{28,24},{5,1},{9,5},{13... | collective-permute-start | bytes 36872 | tf_op jit(solution)/shard_map/ppermute | solution.py:17
Sparse Core Ops, SparseCore 0:
  141.3 33.2 all-gather.1

commit v2 on v1

--- a/solution.py
+++ b/solution.py
@@ -57,26 +57,36 @@
         body(row, lane)
 
 
+def complex_sum(values, real_weights, imag_weights):
+    real = imag = None
+    for value, real_w, imag_w in zip(values, real_weights, imag_weights):
+        real_term, imag_term = value * float(real_w), value * float(imag_w)
+        real = real_term if real is None else real + real_term
+        imag = imag_term if imag is None else imag + imag_term
+    return real, imag
+
+
 def forward_across(x_ref, twiddle_ref, high_ref, low_ref):
     devices, channels, length = x_ref.shape
+    half = devices // 2
     real_w, imag_w = across_weights(devices)
 
     def body(row, lane):
         lanes = pl.ds(lane, lane_step)
+        upper = pl.ds(pl.multiple_of(length + lane, lane_step), lane_step)
         values = [x_ref[m, pl.ds(row, row_step), lanes].astype(jnp.float32) for m in range(devices)]
-        for k in range(devices):
-            real = values[0] * float(real_w[k, 0])
-            imag = None
-            for m in range(1, devices):
-                real = real + values[m] * float(real_w[k, m])
-                term = values[m] * float(imag_w[k, m])
-                imag = term if imag is None else imag + term
-            twiddle_real = twiddle_ref[0, pl.ds(k, 1), lanes]
-            twiddle_imag = twiddle_ref[1, pl.ds(k, 1), lanes]
-            rows = pl.ds(pl.multiple_of(k * channels + row, row_step), row_step)
-            split_store(high_ref, low_ref, rows, lanes, real * twiddle_real - imag * twiddle_imag)
-            upper = pl.ds(pl.multiple_of(length + lane, lane_step), lane_step)
-            split_store(high_ref, low_ref, rows, upper, real * twiddle_imag + imag * twiddle_real)
+        for k in range(half):
+            even = complex_sum(values[::2], real_w[k, ::2], imag_w[k, ::2])
+            odd = complex_sum(values[1::2], real_w[k, 1::2], imag_w[k, 1::2])
+            for at, real, imag in (
+                (k, even[0] + odd[0], even[1] + odd[1]),
+                (k + half, even[0] - odd[0], even[1] - odd[1]),
+            ):
+                twiddle_real = twiddle_ref[0, pl.ds(at, 1), lanes]
+                twiddle_imag = twiddle_ref[1, pl.ds(at, 1), lanes]
+                rows = pl.ds(pl.multiple_of(at * channels + row, row_step), row_step)
+                split_store(high_ref, low_ref, rows, lanes, real * twiddle_real - imag * twiddle_imag)
+                split_store(high_ref, low_ref, rows, upper, real * twiddle_imag + imag * twiddle_real)
 
     tiles_of(channels, length, body)
 
@@ -96,45 +106,70 @@
         )
 
 
-def spectrum_kernel(x_ref, twiddle_ref, table_high_ref, table_low_ref, out_ref, high_ref, low_ref):
+def table_copies(table_refs, held_refs, sems):
+    copies = [
+        pltpu.make_async_copy(table, held, sems.at[i])
+        for i, (table, held) in enumerate(zip(table_refs, held_refs))
+    ]
+    for copy in copies:
+        copy.start()
+    return copies
+
+
+def spectrum_kernel(x_ref, twiddle_ref, table_high, table_low, out_ref, held_high, held_low, sems, high_ref, low_ref):
+    copies = table_copies((table_high, table_low), (held_high, held_low), sems)
     forward_across(x_ref, twiddle_ref, high_ref, low_ref)
-    transform(high_ref, low_ref, table_high_ref, table_low_ref, out_ref)
-
-
-def filter_kernel(sign, x_ref, spectrum_ref, twiddle_ref, table_high_ref, table_low_ref, out_ref, high_ref, low_ref, full_ref):
+    for copy in copies:
+        copy.wait()
+    transform(high_ref, low_ref, held_high, held_low, out_ref)
+
+
+def filter_kernel(
+    sign, x_ref, twiddle_ref, table_high, table_low, spectrum_hbm, out_ref,
+    held_high, held_low, spectrum_ref, sems, high_ref, low_ref, full_ref,
+):
     devices, channels, length = x_ref.shape
+    half = devices // 2
+    copies = table_copies(
+        (table_high, table_low, spectrum_hbm), (held_high, held_low, spectrum_ref), sems
+    )
     forward_across(x_ref, twiddle_ref, high_ref, low_ref)
-    transform(high_ref, low_ref, table_high_ref, table_low_ref, full_ref)
+    for copy in copies:
+        copy.wait()
+    transform(high_ref, low_ref, held_high, held_low, full_ref)
     real_w, imag_w = across_weights(devices)
     scale = 1.0 / (devices * length)
 
-    def multiply(row, lane):
-        rows = pl.ds(row, row_step)
-        lanes = pl.ds(lane, lane_step)
-        upper = pl.ds(pl.multiple_of(length + lane, lane_step), lane_step)
-        data_real, data_imag = full_ref[rows, lanes], full_ref[rows, upper]
-        taps_real, taps_imag = spectrum_ref[rows, lanes], spectrum_ref[rows, upper] * sign
-        split_store(high_ref, low_ref, rows, lanes, data_real * taps_real - data_imag * taps_imag)
-        split_store(high_ref, low_ref, rows, upper, -(data_real * taps_imag + data_imag * taps_real))
-
-    tiles_of(devices * channels, length, multiply)
-    transform(high_ref, low_ref, table_high_ref, table_low_ref, full_ref)
+    @pl.loop(0, devices * channels // row_step)
+    def _(step):
+        rows = pl.ds(pl.multiple_of(step * row_step, row_step), row_step)
+        for lane in range(0, length, lane_step):
+            lanes, upper = pl.ds(lane, lane_step), pl.ds(length + lane, lane_step)
+            data_real, data_imag = full_ref[rows, lanes], full_ref[rows, upper]
+            taps_real, taps_imag = spectrum_ref[rows, lanes], spectrum_ref[rows, upper] * sign
+            split_store(high_ref, low_ref, rows, lanes, data_real * taps_real - data_imag * taps_imag)
+            split_store(high_ref, low_ref, rows, upper, -(data_real * taps_imag + data_imag * taps_real))
+
+    transform(high_ref, low_ref, held_high, held_low, full_ref)
 
     def inverse(row, lane):
         lanes = pl.ds(lane, lane_step)
         upper = pl.ds(pl.multiple_of(length + lane, lane_step), lane_step)
         sums = [None] * devices
-        for k in range(devices):
-            rows = pl.ds(pl.multiple_of(k * channels + row, row_step), row_step)
-            twiddle_real = twiddle_ref[0, pl.ds(k, 1), lanes]
-            twiddle_imag = twiddle_ref[1, pl.ds(k, 1), lanes]
-            real, imag = full_ref[rows, lanes], full_ref[rows, upper]
-            turned_real = real * twiddle_real - imag * twiddle_imag
-            turned_imag = real * twiddle_imag + imag * twiddle_real
+        for k in range(half):
+            turned = []
+            for at in (k, k + half):
+                rows = pl.ds(pl.multiple_of(at * channels + row, row_step), row_step)
+                twiddle_real = twiddle_ref[0, pl.ds(at, 1), lanes]
+                twiddle_imag = twiddle_ref[1, pl.ds(at, 1), lanes]
+                real, imag = full_ref[rows, lanes], full_ref[rows, upper]
+                turned.append((real * twiddle_real - imag * twiddle_imag, real * twiddle_imag + imag * twiddle_real))
+            (near_real, near_imag), (far_real, far_imag) = turned
+            even = (near_real + far_real, near_imag + far_imag)
+            odd = (near_real - far_real, near_imag - far_imag)
             for m in range(devices):
-                term = turned_real * float(scale * real_w[k, m])
-                if m:
-                    term = term - turned_imag * float(scale * imag_w[k, m])
+                real, imag = odd if m % 2 else even
+                term = real * float(scale * real_w[k, m]) - imag * float(scale * imag_w[k, m])
                 sums[m] = term if sums[m] is None else sums[m] + term
         for m in range(devices):
             out_ref[m, pl.ds(row, row_step), lanes] = sums[m].astype(jnp.bfloat16)
@@ -147,33 +182,45 @@
     return jnp.asarray(twiddle_table(devices, length)), jnp.asarray(high), jnp.asarray(low)
 
 
+in_vmem = pl.BlockSpec(memory_space=pltpu.VMEM)
+in_hbm = pl.BlockSpec(memory_space=pltpu.HBM)
+
+
 def spectrum(x, tables):
     devices, channels, length = x.shape
-    rows = devices * channels
+    rows, width = devices * channels, 2 * length
     return pl.pallas_call(
         spectrum_kernel,
-        out_shape=jax.ShapeDtypeStruct((rows, 2 * length), jnp.float32),
-        scratch_shapes=[pltpu.VMEM((rows, 2 * length), jnp.bfloat16)] * 2,
+        out_shape=jax.ShapeDtypeStruct((rows, width), jnp.float32),
+        in_specs=[in_vmem, in_vmem, in_hbm, in_hbm],
+        out_specs=in_vmem,
+        scratch_shapes=[pltpu.VMEM((width, width), jnp.bfloat16)] * 2
+        + [pltpu.SemaphoreType.DMA((2,))]
+        + [pltpu.VMEM((rows, width), jnp.bfloat16)] * 2,
         compiler_params=pltpu.CompilerParams(vmem_limit_bytes=40 << 20),
-        cost_estimate=pl.CostEstimate(
-            flops=6 * rows * (2 * length) ** 2, bytes_accessed=8 << 20, transcendentals=0
-        ),
+        cost_estimate=pl.CostEstimate(flops=6 * rows * width**2, bytes_accessed=8 << 20, transcendentals=0),
     )(x, *tables)
 
 
 def filtered(x, taps_spectrum, tables, sign):
     devices, channels, length = x.shape
-    rows = devices * channels
+    rows, width = devices * channels, 2 * length
     return pl.pallas_call(
         functools.partial(filter_kernel, sign),
         out_shape=jax.ShapeDtypeStruct(x.shape, jnp.bfloat16),
-        scratch_shapes=[pltpu.VMEM((rows, 2 * length), jnp.bfloat16)] * 2
-        + [pltpu.VMEM((rows, 2 * length), jnp.float32)],
+        in_specs=[in_vmem, in_vmem, in_hbm, in_hbm, in_hbm],
+        out_specs=in_vmem,
+        scratch_shapes=[pltpu.VMEM((width, width), jnp.bfloat16)] * 2
+        + [pltpu.VMEM((rows, width), jnp.float32), pltpu.SemaphoreType.DMA((3,))]
+        + [pltpu.VMEM((rows, width), jnp.bfloat16)] * 2
+        + [pltpu.VMEM((rows, width), jnp.float32)],
         compiler_params=pltpu.CompilerParams(vmem_limit_bytes=40 << 20),
-        cost_estimate=pl.CostEstimate(
-            flops=12 * rows * (2 * length) ** 2, bytes_accessed=8 << 20, transcendentals=0
-        ),
-    )(x, taps_spectrum, *tables)
+        cost_estimate=pl.CostEstimate(flops=12 * rows * width**2, bytes_accessed=8 << 20, transcendentals=0),
+    )(x, *tables, taps_spectrum)
+
+
+def swapped(x, axis, bit):
+    return lax.ppermute(x, axis, [(i, i ^ bit) for i in range(lax.axis_size(axis))])
 
 
 def to_channels(x):
@@ -209,14 +256,31 @@
         cotangent, w_out, (((1,), (1,)), ((), ())), preferred_element_type=jnp.float32
     )
     grad_state = grad_gated * conv_q
-    w_columns = lax.all_to_all(w_out, "tp", split_axis=1, concat_axis=0, tiled=True)
+    shares = lax.axis_size("tp")
+    place = lax.axis_index("tp")
+    width = w_out.shape[1] // shares
+    w_pieces = []
+    for bits in range(shares):
+        piece = lax.dynamic_slice_in_dim(w_out, (place ^ bits) * width, width, 1)
+        w_pieces.append(swapped(piece, "tp", bits) if bits else piece)
     taps_spectrum = spectrum(taps_channels, tables)
-    mixer_state = to_positions(filtered(to_channels(source), taps_spectrum, tables, 1.0)) + skip_gain * source
+    state_channels = filtered(to_channels(source), taps_spectrum, tables, 1.0)
+    grad_channels, w_pieces = lax.optimization_barrier((to_channels(grad_state), w_pieces))
+    mixer_state = to_positions(state_channels) + skip_gain * source
     gated = (conv_q * mixer_state).astype(jnp.bfloat16)
-    all_gated = lax.all_gather(gated, "tp", axis=1, tiled=True)
-    mixed = jnp.dot(all_gated, w_columns, preferred_element_type=jnp.float32).astype(jnp.bfloat16)
+    pieces = {0: gated}
+    bit = shares // 2
+    while bit:
+        order = sorted(pieces)
+        received = swapped(jnp.stack([pieces[i] for i in order]), "tp", bit)
+        pieces.update({i ^ bit: received[at] for at, i in enumerate(order)})
+        bit //= 2
+    total = sum(
+        jnp.dot(pieces[i], w_pieces[i], preferred_element_type=jnp.float32) for i in range(shares)
+    )
+    mixed = total.astype(jnp.bfloat16)
     grad_q = grad_gated * mixer_state
-    grad_source = to_positions(filtered(to_channels(grad_state), taps_spectrum, tables, -1.0)) + skip_gain * grad_state
+    grad_source = to_positions(filtered(grad_channels, taps_spectrum, tables, -1.0)) + skip_gain * grad_state
     gradients = jnp.stack([grad_q, grad_source * conv_v, grad_source * conv_k])
     following = passed_along(gradients[:, :2, :], "seq", -1)
     grad_ext = jnp.concatenate([gradients, following], axis=1)

time: 211 us -> 170 us (0.81)
  between operations: 14.3 us -> 0.96 us
  local copies, waits for them, and re-layouts: 32.5 us -> 21.2 us
  waiting for transfers between devices: 66.4 us -> 58.2 us
  Pallas kernels: 34.9 us -> 30.6 us
  other arithmetic: 14.6 us -> 12.2 us
    all_to_all x1 -> x0, waiting for transfers between devices: 39.4 us -> none  [on_device(): lax.all_to_all(w_out, 'tp', split_axis=1, concat_axis=0, tiled=True)]
    ppermute x0 -> x5, waiting for transfers between devices: none -> 29.8 us  [swapped(): lax.ppermute(x, axis, [(i, i ^ bit) for i in range(lax.axis_size(axis))])]
    unnamed x37 -> x34, local copies, waits for them, and re-layouts: 18.5 us -> 7.8 us
    all_to_all x1 -> x0, local copies, waits for them, and re-layouts: 6.29 us -> none  [on_device(): lax.all_to_all(w_out, 'tp', split_axis=1, concat_axis=0, tiled=True)]
    all_to_all x2, waiting for transfers between devices: 5.56 us -> 11.1 us  [to_positions(): lax.all_to_all(x.reshape(devices * channels, length), 'seq', split_axis=0...]
    all_to_all x1 -> x0, starting transfers between devices: 4.89 us -> none  [on_device(): lax.all_to_all(w_out, 'tp', split_axis=1, concat_axis=0, tiled=True)]
    dynamic_slice x0 -> x1, local copies, waits for them, and re-layouts: none -> 4.43 us  [on_device(): piece = lax.dynamic_slice_in_dim(w_out, (place ^ bits) * width, width, 1)]
    pallas_call x2, Pallas kernels: 29.3 us -> 25 us  [filtered(): pl.pallas_call(functools.partial(filter_kernel, sign), out_shape=jax.Shap...]
  transfers between devices with their start and end apart: 9 -> 12, of which waited for: 5 -> 5; matrix products, arithmetic and copies ran while one was open for 19% -> 15% of each run, Pallas kernels for 17% -> 18%
where the time goes in v2:
time: 170 us
  waiting for transfers between devices  58.2 us (34%)
  starting transfers between devices  33.8 us (20%)
  Pallas kernels  30.6 us (18%)
  local copies, waits for them, and re-layouts  21.2 us (12%)
  matrix products  12.5 us (7%)
  other arithmetic  12.2 us (7%)
    ppermute x5, waiting for transfers between devices, swapped(): lax.ppermute(x, axis, [(i, i ^ bit) for i in range(lax.axis_size(axis))])  29.8 us
    pallas_call x2, Pallas kernels, filtered(): pl.pallas_call(functools.partial(filter_kernel, sign), out_shape=jax.Shap...  25 us
    all_to_all x3, waiting for transfers between devices, to_channels(): lax.all_to_all(turned, 'seq', split_axis=0, concat_axis=0, tiled=True)  17.2 us
    all_to_all x3, starting transfers between devices, to_channels(): lax.all_to_all(turned, 'seq', split_axis=0, concat_axis=0, tiled=True)  12.1 us
    all_to_all x2, starting transfers between devices, to_positions(): lax.all_to_all(x.reshape(devices * channels, length), 'seq', split_axis=0...  12 us
    all_to_all x2, waiting for transfers between devices, to_positions(): lax.all_to_all(x.reshape(devices * channels, length), 'seq', split_axis=0...  11.1 us
    unnamed x34, local copies, waits for them, and re-layouts  7.8 us
    dot_general x4, matrix products, on_device(): jnp.dot(pieces[i], w_pieces[i], preferred_element_type=jnp.float32)  6.57 us
  transfers between devices with their start and end apart: 12, of which 5 were waited for; matrix products, arithmetic and copies ran while one was open for 15% of the time, Pallas kernels for 18%

profile of v2, /device:TPU:0, one launch (start us, length us, event | category | flops | bytes accessed | tf_op | source)
XLA Modules:
  0.0 169.5 jit_solution(2456978897384975003)
XLA Ops:
  0.6 0.8 slice.49
  1.4 4.8 %collective-permute-start = (bf16[3,2,512]{2,1,0:T(2,128)(2,1)S(1)}, bf16[3,2,512]{2,1,0:T(2,128)(2,1)S(1)}, u32[]{:S(2)}, u32[]{:S(2)}) collective-permute-start(bf16[3,2,512]{2,1,0:T(2,128)(2,1)S(1)} %slice.49), channel_id=1, source_target_pairs={{0,4},{4,8},{8,12},{12,16},{16,20},{20,24},{24,28},{1,5},{5,9},{9,... | collective-permute-start | bytes 18440 | tf_op jit(solution)/shard_map/ppermute | solution.py:17
  6.2 1.3 convert_bitcast_fusion.1
  7.5 1.0 copy.17
  8.5 4.9 %all-to-all-start.1 = ((bf16[8,64,512]{2,1,0:T(8,128)(2,1)}), bf16[8,64,512]{2,1,0:T(8,128)(2,1)S(1)}, u32[]{:S(2)}, u32[]{:S(2)}) async-start(bf16[8,64,512]{2,1,0:T(8,128)(2,1)} %bitcast.6), calls=%async_computation.1 | async-start | bytes 1048576 | tf_op jit(solution)/shard_map/all_to_all | solution.py:229
  13.5 5.9 %fusion.12 = f32[512,512]{1,0:T(8,128)S(1)} fusion(bf16[512,4096]{1,0:T(8,128)(2,1)} %param.14, bf16[512,4096]{1,0:T(8,128)(2,1)} %param.13), kind=kOutput, calls=%fused_computation.45 | convolution fusion | flops 2147483648 | bytes 9437184 | tf_op jit(solution)/shard_map/dot_general | solution.py:255
  19.5 0.5 maximum_convert_fusion
  19.9 0.9 fusion.3
  20.9 1.6 copy-done.7
  22.5 0.4 convert_bitcast_fusion.2
  22.9 1.0 copy.16
  23.9 3.8 %all-to-all-done.1.x_ref = bf16[8,64,512]{2,1,0:T(8,128)(2,1)S(1)} async-done(((bf16[8,64,512]{2,1,0:T(8,128)(2,1)}), bf16[8,64,512]{2,1,0:T(8,128)(2,1)S(1)}, u32[]{:S(2)}, u32[]{:S(2)}) %all-to-all-start.1) | async-done | bytes 524320 | tf_op jit(solution)/shard_map/all_to_all | solution.py:229
  27.7 3.6 %all-to-all-start = ((bf16[8,64,512]{2,1,0:T(8,128)(2,1)}), bf16[8,64,512]{2,1,0:T(8,128)(2,1)S(1)}, u32[]{:S(2)}, u32[]{:S(2)}) async-start(bf16[8,64,512]{2,1,0:T(8,128)(2,1)} %bitcast.4), calls=%async_computation | async-start | bytes 1048576 | tf_op jit(solution)/shard_map/all_to_all | solution.py:229
  31.3 1.0 copy.19
  32.3 13.5 %all-to-all-done.x_ref = bf16[8,64,512]{2,1,0:T(8,128)(2,1)S(1)} async-done(((bf16[8,64,512]{2,1,0:T(8,128)(2,1)}), bf16[8,64,512]{2,1,0:T(8,128)(2,1)S(1)}, u32[]{:S(2)}, u32[]{:S(2)}) %all-to-all-start) | async-done | bytes 524320 | tf_op jit(solution)/shard_map/all_to_all | solution.py:229
  45.8 3.6 %all-to-all-start.3 = ((bf16[8,64,512]{2,1,0:T(8,128)(2,1)}), bf16[8,64,512]{2,1,0:T(8,128)(2,1)S(1)}, u32[]{:S(2)}, u32[]{:S(2)}) async-start(bf16[8,64,512]{2,1,0:T(8,128)(2,1)} %bitcast.10), calls=%async_computation.3 | async-start | bytes 1048576 | tf_op jit(solution)/shard_map/all_to_all | solution.py:229
  49.4 4.4 %constant_dynamic-slice_fusion = (bf16[512,1024]{1,0:T(8,128)(2,1)}, bf16[512,1024]{1,0:T(8,128)(2,1)}, bf16[512,1024]{1,0:T(8,128)(2,1)}, bf16[512,1024]{1,0:T(8,128)(2,1)}) fusion(bf16[512,4096]{1,0:T(8,128)(2,1)} %param.13, s32[]{:T(128)S(6)} %select_n.15, s32[]{:T(128)S(6)} %select_n.13, s32[]{:T(128)S(6)} %select_n.12, s32[]{:T(128)S(6)} %select_n.14), kind=kLoop, calls=%fused_computation.40 | loop fusion | bytes 8388624 | tf_op jit(solution)/shard_map/dynamic_slice | solution.py:264
  53.9 1.5 collective-permute-start.2
  55.4 0.3 collective-permute-start.3
  55.7 5.6 %shard_map.104.spectrum_hbm = f32[512,1024]{1,0:T(8,128)S(1)} custom-call(bf16[8,64,512]{2,1,0:T(8,128)(2,1)S(1)} %all-to-all-done.1.x_ref, f32[2,8,512]{2,1,0:T(8,128)S(1)} %copy-done.4, bf16[1024,1024]{1,0:T(8,128)(2,1)S(1)} %copy-done, bf16[1024,1024]{1,0:T(8,128)(2,1)S(1)} %copy-done.2), custom_call_target="tpu_custom_call" | custom-call | flops 3221225472 | bytes 8388608 | tf_op jit(solution)/shard_map/pallas_call | solution.py:192
  61.4 12.5 %shard_map.105 = bf16[8,64,512]{2,1,0:T(8,128)(2,1)} custom-call(bf16[8,64,512]{2,1,0:T(8,128)(2,1)S(1)} %all-to-all-done.x_ref, f32[2,8,512]{2,1,0:T(8,128)S(1)} %copy-done.4, bf16[1024,1024]{1,0:T(8,128)(2,1)S(1)} %copy-done, bf16[1024,1024]{1,0:T(8,128)(2,1)S(1)} %copy-done.2, f32[512,1024]{1,0:T(8,128)S(1)} %shard_map.104.spectrum_hbm), custom_call_target="tpu_custom_call" | custom-call | flops 6442450944 | bytes 8388608 | tf_op jit(solution)/shard_map/pallas_call | solution.py:208
  73.9 1.3 copy-done.5
  75.2 6.0 %all-to-all-start.2 = ((bf16[8,64,512]{2,1,0:T(8,128)(2,1)}), bf16[8,64,512]{2,1,0:T(8,128)(2,1)S(1)}, u32[]{:S(2)}, u32[]{:S(2)}) async-start(bf16[8,64,512]{2,1,0:T(8,128)(2,1)} %shard_map.105), calls=%async_computation.2 | async-start | bytes 1048576 | tf_op jit(solution)/shard_map/all_to_all | solution.py:235
  81.2 20.6 %collective-permute-done.3 = bf16[512,1024]{1,0:T(8,128)(2,1)} collective-permute-done((bf16[512,1024]{1,0:T(8,128)(2,1)}, bf16[512,1024]{1,0:T(8,128)(2,1)}, u32[]{:S(2)}, u32[]{:S(2)}) %collective-permute-start.3) | collective-permute-done | bytes 1048608 | tf_op jit(solution)/shard_map/ppermute | solution.py:223
  101.9 1.6 copy-done.1
  103.4 1.6 copy-done.3
  105.0 1.6 copy-done.6
  106.6 12.5 %shard_map.106 = bf16[8,64,512]{2,1,0:T(8,128)(2,1)} custom-call(bf16[8,64,512]{2,1,0:T(8,128)(2,1)S(1)} %all-to-all-done.3.x_ref, f32[2,8,512]{2,1,0:T(8,128)S(1)} %copy-done.4, bf16[1024,1024]{1,0:T(8,128)(2,1)S(1)} %copy-done.1, bf16[1024,1024]{1,0:T(8,128)(2,1)S(1)} %copy-done.3, f32[512,1024]{1,0:T(8,128)S(1)} %copy-done.6), custom_call_target="tpu_custom_call" | custom-call | flops 6442450944 | bytes 8388608 | tf_op jit(solution)/shard_map/pallas_call | solution.py:208
  119.1 6.0 %all-to-all-start.4 = ((bf16[8,64,512]{2,1,0:T(8,128)(2,1)}), bf16[8,64,512]{2,1,0:T(8,128)(2,1)}, u32[]{:S(2)}, u32[]{:S(2)}) async-start(bf16[8,64,512]{2,1,0:T(8,128)(2,1)} %shard_map.106), calls=%async_computation.4 | async-start | bytes 1048576 | tf_op jit(solution)/shard_map/all_to_all | solution.py:235
  125.1 1.1 bitcast_convert_fusion.1
  126.3 2.7 %copy.18 = f32[512,512]{0,1:T(8,128)} copy(f32[512,512]{1,0:T(8,128)} %bitcast_convert_fusion.1) | data formatting | bytes 2097152 | tf_op jit(solution)/shard_map/convert_element_type | solution.py:236
  129.0 11.1 %all-to-all-done.4 = bf16[8,64,512]{2,1,0:T(8,128)(2,1)} async-done(((bf16[8,64,512]{2,1,0:T(8,128)(2,1)}), bf16[8,64,512]{2,1,0:T(8,128)(2,1)}, u32[]{:S(2)}, u32[]{:S(2)}) %all-to-all-start.4) | async-done | bytes 524320 | tf_op jit(solution)/shard_map/all_to_all | solution.py:235
  140.1 2.1 %bitcast_convert_fusion = f32[512,512]{1,0:T(8,128)} fusion(bf16[8,64,512]{2,1,0:T(8,128)(2,1)} %all-to-all-done.4), kind=kLoop, calls=%fused_computation.30 | loop fusion | flops 262144 | bytes 1572864 | tf_op jit(solution)/shard_map/convert_element_type | solution.py:236
  142.2 2.5 %copy.20 = f32[512,512]{0,1:T(8,128)} copy(f32[512,512]{1,0:T(8,128)} %bitcast_convert_fusion) | data formatting | bytes 2097152 | tf_op jit(solution)/shard_map/convert_element_type | solution.py:236
  144.8 2.7 %multiply_bitcast_fusion.2 = (f32[1,512,512]{2,1,0:T(8,128)S(1)}, bf16[512,512]{1,0:T(8,128)(2,1)S(1)}, f32[1,512,512]{2,1,0:T(8,128)S(1)}, f32[512,512]{1,0:T(8,128)S(1)}) fusion(f32[512,512]{1,0:T(8,128)} %copy-done.10, f32[512]{0:T(512)S(1)} %copy-done.15, f32[512,512]{0,1:T(8,128)} %copy.18, f32[3,512,512]{2,1,0:T(8,128)S(1)} %copy-done.8, ...), kind=kLoop, calls=%fused_computation.22 | loop fusion | flops 2621440 | bytes 9963520 | tf_op jit(solution)/shard_map/stack | solution.py:284
  147.4 1.6 collective-permute-start.4
  149.0 0.2 multiply_bitcast_fusion
  149.3 0.3 pad_maximum_fusion.1
  149.6 1.3 collective-permute-start.6
  150.9 9.2 %collective-permute-done.4 = bf16[1,512,512]{2,1,0:T(8,128)(2,1)S(1)} collective-permute-done((bf16[1,512,512]{2,1,0:T(8,128)(2,1)S(1)}, bf16[1,512,512]{2,1,0:T(8,128)(2,1)S(1)}, u32[]{:S(2)}, u32[]{:S(2)}) %collective-permute-start.4) | collective-permute-done | bytes 524320 | tf_op jit(solution)/shard_map/ppermute | solution.py:223
  160.1 0.1 pad_maximum_fusion.2
  160.2 0.1 collective-permute-start.5
  160.3 0.7 fusion.13
  161.0 0.4 pad_maximum_fusion
  161.4 2.2 %fusion.1 = bf16[3,512,512]{2,1,0:T(8,128)(2,1)} fusion(f32[3,514,512]{2,1,0:T(8,128)S(1)} %pad_maximum_fusion, f32[3,512]{1,0:T(4,128)S(1)} %get-tuple-element.27, f32[3,512]{1,0:T(4,128)S(1)} %get-tuple-element.28, f32[3,512]{1,0:T(4,128)S(1)} %bitcast.94, f32[1,512,512]{2,1,0:T(8,128)S(1)} %multiply_bitcast_fusion, ...), kind=kLoop, calls=%fused_computation.3 | loop fusion | flops 6291456 | bytes 11028480 | tf_op jit(solution)/shard_map/convert_element_type | solution.py:292
  163.6 2.0 %fusion.9 = f32[512,1024]{1,0:T(8,128)S(1)} fusion(bf16[512,1024]{1,0:T(8,128)(2,1)} %collective-permute-done.2, bf16[1,512,512]{2,1,0:T(8,128)(2,1)S(1)} %collective-permute-done.4), kind=kOutput, calls=%fused_computation.32 | convolution fusion | flops 536870912 | bytes 3670016 | tf_op jit(solution)/shard_map/dot_general | solution.py:279
  165.7 0.7 fusion.8
  166.4 3.1 %add_convert_fusion = bf16[512,1024]{1,0:T(8,128)(2,1)} fusion(f32[512,1024]{1,0:T(8,128)S(1)} %fusion.9, f32[512,1024]{1,0:T(8,128)S(1)} %fusion.13, f32[512,1024]{1,0:T(8,128)S(1)} %fusion.8, bf16[512,1024]{1,0:T(8,128)(2,1)} %collective-permute-done.3, bf16[2,512,512]{2,1,0:T(8,128)(2,1)S(1)} %collective-permute-done.5), kind=kOutput, calls=%fused_computation.12 | convolution fusion | flops 538968064 | bytes 8912896 | tf_op jit(solution)/shard_map/dot_general | solution.py:279
  (39 shorter events, 0.1 us)
Async XLA Ops:
  0.6 12.8 %copy-start.14 = (f32[3,3,512]{2,1,0:T(4,128)S(1)}, f32[3,3,512]{2,1,0:T(4,128)}, u32[]{:S(2)}) copy-start(f32[3,3,512]{2,1,0:T(4,128)} %param.10) | copy-start | bytes 55300
  1.4 18.0 %collective-permute-start = (bf16[3,2,512]{2,1,0:T(2,128)(2,1)S(1)}, bf16[3,2,512]{2,1,0:T(2,128)(2,1)S(1)}, u32[]{:S(2)}, u32[]{:S(2)}) collective-permute-start(bf16[3,2,512]{2,1,0:T(2,128)(2,1)S(1)} %slice.49), channel_id=1, source_target_pairs={{0,4},{4,8},{8,12},{12,16},{16,20},{20,24},{24,28},{1,5},{5,9},{9,... | collective-permute-start | bytes 18440 | tf_op jit(solution)/shard_map/ppermute | solution.py:17
  8.5 19.1 %all-to-all-start.1 = ((bf16[8,64,512]{2,1,0:T(8,128)(2,1)}), bf16[8,64,512]{2,1,0:T(8,128)(2,1)S(1)}, u32[]{:S(2)}, u32[]{:S(2)}) async-start(bf16[8,64,512]{2,1,0:T(8,128)(2,1)} %bitcast.6), calls=%async_computation.1 | async-start | bytes 1048576 | tf_op jit(solution)/shard_map/all_to_all | solution.py:229
  13.5 6.0 %copy-start.11 = (bf16[3,512,512]{2,1,0:T(8,128)(2,1)S(1)}, bf16[3,512,512]{2,1,0:T(8,128)(2,1)}, u32[]{:S(2)}) copy-start(bf16[3,512,512]{2,1,0:T(8,128)(2,1)} %param.9) | copy-start | bytes 4718596
  19.4 1.5 copy-start.10
  20.9 1.6 copy-start.7
  27.7 18.1 %all-to-all-start = ((bf16[8,64,512]{2,1,0:T(8,128)(2,1)}), bf16[8,64,512]{2,1,0:T(8,128)(2,1)S(1)}, u32[]{:S(2)}, u32[]{:S(2)}) async-start(bf16[8,64,512]{2,1,0:T(8,128)(2,1)} %bitcast.4), calls=%async_computation | async-start | bytes 1048576 | tf_op jit(solution)/shard_map/all_to_all | solution.py:229
  45.8 29.4 %all-to-all-start.3 = ((bf16[8,64,512]{2,1,0:T(8,128)(2,1)}), bf16[8,64,512]{2,1,0:T(8,128)(2,1)S(1)}, u32[]{:S(2)}, u32[]{:S(2)}) async-start(bf16[8,64,512]{2,1,0:T(8,128)(2,1)} %bitcast.10), calls=%async_computation.3 | async-start | bytes 1048576 | tf_op jit(solution)/shard_map/all_to_all | solution.py:229
  49.4 6.3 %copy-start = (bf16[1024,1024]{1,0:T(8,128)(2,1)S(1)}, bf16[1024,1024]{1,0:T(8,128)(2,1)}, u32[]{:S(2)}) copy-start(bf16[1024,1024]{1,0:T(8,128)(2,1)} %constant.23.clone.table_high) | copy-start | bytes 6291460
  49.4 6.3 %copy-start.2 = (bf16[1024,1024]{1,0:T(8,128)(2,1)S(1)}, bf16[1024,1024]{1,0:T(8,128)(2,1)}, u32[]{:S(2)}) copy-start(bf16[1024,1024]{1,0:T(8,128)(2,1)} %constant.24.clone.table_low) | copy-start | bytes 6291460
  49.4 6.3 %copy-start.4 = (f32[2,8,512]{2,1,0:T(8,128)S(1)}, f32[2,8,512]{2,1,0:T(8,128)}, u32[]{:S(2)}) copy-start(f32[2,8,512]{2,1,0:T(8,128)} %constant.22.clone.twiddle_ref) | copy-start | bytes 98308
  53.9 27.3 %collective-permute-start.1 = (bf16[512,1024]{1,0:T(8,128)(2,1)}, bf16[512,1024]{1,0:T(8,128)(2,1)S(1)}, u32[]{:S(2)}, u32[]{:S(2)}) collective-permute-start(bf16[512,1024]{1,0:T(8,128)(2,1)} %get-tuple-element.19), channel_id=1, source_target_pairs={{0,1},{1,0},{2,3},{3,2},{4,5},{5,4},{6,7},{7,6},{8,9},{9,8},{10,11... | collective-permute-start | bytes 3145736 | tf_op jit(solution)/shard_map/ppermute | solution.py:223
  53.9 27.4 %collective-permute-start.2 = (bf16[512,1024]{1,0:T(8,128)(2,1)}, bf16[512,1024]{1,0:T(8,128)(2,1)}, u32[]{:S(2)}, u32[]{:S(2)}) collective-permute-start(bf16[512,1024]{1,0:T(8,128)(2,1)} %get-tuple-element.21), channel_id=1, source_target_pairs={{0,2},{1,3},{2,0},{3,1},{4,6},{5,7},{6,4},{7,5},{8,10},{9,11},{10,... | collective-permute-start | bytes 3145736 | tf_op jit(solution)/shard_map/ppermute | solution.py:223
  55.4 46.4 %collective-permute-start.3 = (bf16[512,1024]{1,0:T(8,128)(2,1)}, bf16[512,1024]{1,0:T(8,128)(2,1)}, u32[]{:S(2)}, u32[]{:S(2)}) collective-permute-start(bf16[512,1024]{1,0:T(8,128)(2,1)} %get-tuple-element.18), channel_id=1, source_target_pairs={{0,3},{1,2},{2,1},{3,0},{4,7},{5,6},{6,5},{7,4},{8,11},{9,10},{10,... | collective-permute-start | bytes 3145736 | tf_op jit(solution)/shard_map/ppermute | solution.py:223
  73.9 1.3 copy-start.5
  75.2 43.9 %all-to-all-start.2 = ((bf16[8,64,512]{2,1,0:T(8,128)(2,1)}), bf16[8,64,512]{2,1,0:T(8,128)(2,1)S(1)}, u32[]{:S(2)}, u32[]{:S(2)}) async-start(bf16[8,64,512]{2,1,0:T(8,128)(2,1)} %shard_map.105), calls=%async_computation.2 | async-start | bytes 1048576 | tf_op jit(solution)/shard_map/all_to_all | solution.py:235
  81.2 37.9 %copy-start.12 = (bf16[512,1024]{1,0:T(8,128)(2,1)}, bf16[512,1024]{1,0:T(8,128)(2,1)S(1)}, u32[]{:S(2)}) copy-start(bf16[512,1024]{1,0:T(8,128)(2,1)S(1)} %collective-permute-done.1) | copy-start | bytes 3145732
  101.8 1.6 copy-start.1
  103.4 1.6 copy-start.3
  105.0 1.6 copy-start.6
  119.1 21.0 %all-to-all-start.4 = ((bf16[8,64,512]{2,1,0:T(8,128)(2,1)}), bf16[8,64,512]{2,1,0:T(8,128)(2,1)}, u32[]{:S(2)}, u32[]{:S(2)}) async-start(bf16[8,64,512]{2,1,0:T(8,128)(2,1)} %shard_map.106), calls=%async_computation.4 | async-start | bytes 1048576 | tf_op jit(solution)/shard_map/all_to_all | solution.py:235
  126.3 18.5 %copy-start.8 = (f32[3,512,512]{2,1,0:T(8,128)S(1)}, f32[3,512,512]{2,1,0:T(8,128)}, u32[]{:S(2)}) copy-start(f32[3,512,512]{2,1,0:T(8,128)} %copy-done.7) | copy-start | bytes 9437188
  126.3 18.5 %copy-start.15 = (f32[512]{0:T(512)S(1)}, f32[512]{0:T(512)}, u32[]{:S(2)}) copy-start(f32[512]{0:T(512)} %param.12) | copy-start | bytes 6148
  147.4 12.7 %collective-permute-start.4 = (bf16[1,512,512]{2,1,0:T(8,128)(2,1)S(1)}, bf16[1,512,512]{2,1,0:T(8,128)(2,1)S(1)}, u32[]{:S(2)}, u32[]{:S(2)}) collective-permute-start(bf16[1,512,512]{2,1,0:T(8,128)(2,1)S(1)} %bitcast.91), channel_id=1, source_target_pairs={{0,2},{1,3},{2,0},{3,1},{4,6},{5,7},{6,4},{7,5},{8,10},{9,11},{10,... | collective-permute-start | bytes 1572872 | tf_op jit(solution)/shard_map/ppermute | solution.py:223
  149.3 11.0 %copy-start.9 = (bf16[512,1024]{1,0:T(8,128)(2,1)S(1)}, bf16[512,1024]{1,0:T(8,128)(2,1)}, u32[]{:S(2)}) copy-start(bf16[512,1024]{1,0:T(8,128)(2,1)} %get-tuple-element.7) | copy-start | bytes 3145732
  149.6 11.4 %collective-permute-start.6 = (f32[3,2,512]{2,1,0:T(2,128)S(1)}, f32[3,2,512]{2,1,0:T(2,128)S(1)}, u32[]{:S(2)}, u32[]{:S(2)}) collective-permute-start(f32[3,2,512]{2,1,0:T(2,128)S(1)} %slice.71), channel_id=1, source_target_pairs={{4,0},{8,4},{12,8},{16,12},{20,16},{24,20},{28,24},{5,1},{9,5},{13... | collective-permute-start | bytes 36872 | tf_op jit(solution)/shard_map/ppermute | solution.py:17
  160.2 5.5 %collective-permute-start.5 = (bf16[2,512,512]{2,1,0:T(8,128)(2,1)S(1)}, bf16[2,512,512]{2,1,0:T(8,128)(2,1)S(1)}, u32[]{:S(2)}, u32[]{:S(2)}) collective-permute-start(bf16[2,512,512]{2,1,0:T(8,128)(2,1)S(1)} %pad_maximum_fusion.2), channel_id=1, source_target_pairs={{0,1},{1,0},{2,3},{3,2},{4,5},{5,4},{6,7},{7,6},{8,9},{9,8},{10,11... | collective-permute-start | bytes 3145736 | tf_op jit(solution)/shard_map/ppermute | solution.py:223
  163.6 2.1 %copy-start.13 = (bf16[512,1024]{1,0:T(8,128)(2,1)S(1)}, bf16[512,1024]{1,0:T(8,128)(2,1)}, u32[]{:S(2)}) copy-start(bf16[512,1024]{1,0:T(8,128)(2,1)} %copy-done.12) | copy-start | bytes 3145732

commit v3 on v2

--- a/solution.py
+++ b/solution.py
@@ -197,7 +197,7 @@
         scratch_shapes=[pltpu.VMEM((width, width), jnp.bfloat16)] * 2
         + [pltpu.SemaphoreType.DMA((2,))]
         + [pltpu.VMEM((rows, width), jnp.bfloat16)] * 2,
-        compiler_params=pltpu.CompilerParams(vmem_limit_bytes=40 << 20),
+        compiler_params=pltpu.CompilerParams(vmem_limit_bytes=58 << 20),
         cost_estimate=pl.CostEstimate(flops=6 * rows * width**2, bytes_accessed=8 << 20, transcendentals=0),
     )(x, *tables)
 
@@ -214,7 +214,7 @@
         + [pltpu.VMEM((rows, width), jnp.float32), pltpu.SemaphoreType.DMA((3,))]
         + [pltpu.VMEM((rows, width), jnp.bfloat16)] * 2
         + [pltpu.VMEM((rows, width), jnp.float32)],
-        compiler_params=pltpu.CompilerParams(vmem_limit_bytes=40 << 20),
+        compiler_params=pltpu.CompilerParams(vmem_limit_bytes=58 << 20),
         cost_estimate=pl.CostEstimate(flops=12 * rows * width**2, bytes_accessed=8 << 20, transcendentals=0),
     )(x, *tables, taps_spectrum)
 
@@ -223,24 +223,26 @@
     return lax.ppermute(x, axis, [(i, i ^ bit) for i in range(lax.axis_size(axis))])
 
 
-def to_channels(x):
+def to_channels(turned):
     devices = lax.axis_size("seq")
-    turned = x.astype(jnp.bfloat16).T
     moved = lax.all_to_all(turned, "seq", split_axis=0, concat_axis=0, tiled=True)
-    return moved.reshape(devices, x.shape[1] // devices, x.shape[0])
+    return moved.reshape(devices, turned.shape[0] // devices, turned.shape[1])
+
+
+def turned_over(x):
+    return x.astype(jnp.bfloat16).T
 
 
 def to_positions(x):
     devices, channels, length = x.shape
-    moved = lax.all_to_all(x.reshape(devices * channels, length), "seq", split_axis=0, concat_axis=0, tiled=True)
-    return moved.T.astype(jnp.float32)
+    return lax.all_to_all(x.reshape(devices * channels, length), "seq", split_axis=0, concat_axis=0, tiled=True)
 
 
 def on_device(streams, short_taps, filter_taps, skip_gain, w_out, cotangent):
     length = streams.shape[1]
     devices = lax.axis_size("seq")
     tables = tables_for(devices, length)
-    taps_channels = to_channels(filter_taps)
+    taps_channels = to_channels(turned_over(filter_taps))
     previous = passed_along(streams[:, -2:, :], "seq", 1)
     extended = jnp.concatenate([previous, streams], axis=1).astype(jnp.float32)
     convolved = (
@@ -264,9 +266,18 @@
         piece = lax.dynamic_slice_in_dim(w_out, (place ^ bits) * width, width, 1)
         w_pieces.append(swapped(piece, "tp", bits) if bits else piece)
     taps_spectrum = spectrum(taps_channels, tables)
-    state_channels = filtered(to_channels(source), taps_spectrum, tables, 1.0)
-    grad_channels, w_pieces = lax.optimization_barrier((to_channels(grad_state), w_pieces))
-    mixer_state = to_positions(state_channels) + skip_gain * source
+    grad_turned, taps_spectrum = lax.optimization_barrier((turned_over(grad_state), taps_spectrum))
+    early = 2 % shares
+    source_channels, w_pieces[early] = lax.optimization_barrier(
+        (to_channels(turned_over(source)), w_pieces[early])
+    )
+    state_channels = filtered(source_channels, taps_spectrum, tables, 1.0)
+    state_channels, grad_received = lax.optimization_barrier((state_channels, to_channels(grad_turned)))
+    grad_channels = filtered(grad_received, taps_spectrum, tables, -1.0)
+    state_positions, grad_channels, w_pieces = lax.optimization_barrier(
+        (to_positions(state_channels), grad_channels, w_pieces)
+    )
+    mixer_state = state_positions.T.astype(jnp.float32) + skip_gain * source
     gated = (conv_q * mixer_state).astype(jnp.bfloat16)
     pieces = {0: gated}
     bit = shares // 2
@@ -280,7 +291,8 @@
     )
     mixed = total.astype(jnp.bfloat16)
     grad_q = grad_gated * mixer_state
-    grad_source = to_positions(filtered(grad_channels, taps_spectrum, tables, -1.0)) + skip_gain * grad_state
+    grad_positions, mixed = lax.optimization_barrier((to_positions(grad_channels), mixed))
+    grad_source = grad_positions.T.astype(jnp.float32) + skip_gain * grad_state
     gradients = jnp.stack([grad_q, grad_source * conv_v, grad_source * conv_k])
     following = passed_along(gradients[:, :2, :], "seq", -1)
     grad_ext = jnp.concatenate([gradients, following], axis=1)

time: 170 us -> 147 us (0.86)
  waiting for transfers between devices: 58.2 us -> 27.8 us
  Pallas kernels: 30.6 us -> 38 us
  local copies, waits for them, and re-layouts: 21.2 us -> 14.6 us
  matrix products: 12.5 us -> 16.2 us
  starting transfers between devices: 33.8 us -> 36.7 us
    all_to_all x3, waiting for transfers between devices: 17.2 us -> 2.22 us  [to_channels(): lax.all_to_all(turned, 'seq', split_axis=0, concat_axis=0, tiled=True)]
    ppermute x5, waiting for transfers between devices: 29.8 us -> 15.4 us  [swapped(): lax.ppermute(x, axis, [(i, i ^ bit) for i in range(lax.axis_size(axis))])]
    unnamed x34 -> x16, local copies, waits for them, and re-layouts: 7.8 us -> 0.33 us
    optimization_barrier x0 -> x3, local copies, waits for them, and re-layouts: none -> 6.14 us  [the longest x1 2.05 us: on_device(): lax.optimization_barrier((turned_over(grad_state), taps_spectrum))]
    convert_element_type x2 -> x0, local copies, waits for them, and re-layouts: 5.23 us -> none  [to_positions(): return moved.T.astype(jnp.float32)]
    all_to_all x2, waiting for transfers between devices: 11.1 us -> 5.92 us  [to_positions(): lax.all_to_all(x.reshape(devices * channels, length), 'seq', split_axis=0...]
    pallas_call x2, Pallas kernels: 25 us -> 29.3 us  [filtered(): pl.pallas_call(functools.partial(filter_kernel, sign), out_shape=jax.Shap...]
    ppermute x2, waiting for transfers between devices: 0.01 us -> 4.29 us  [passed_along(): return lax.ppermute(x, axis, pairs)]
  transfers between devices with their start and end apart: 12 -> 12, of which waited for: 5 -> 5; matrix products, arithmetic and copies ran while one was open for 15% -> 20% of each run, Pallas kernels for 18% -> 26%
where the time goes in v3:
time: 147 us; the launch traced here: 146 us
  Pallas kernels  38 us (26%)
  starting transfers between devices  36.7 us (25%)
  waiting for transfers between devices  27.8 us (19%)
  matrix products  16.2 us (11%)
  local copies, waits for them, and re-layouts  14.6 us (10%)
  other arithmetic  11.7 us (8%)
    pallas_call x2, Pallas kernels, filtered(): pl.pallas_call(functools.partial(filter_kernel, sign), out_shape=jax.Shap...  29.3 us
    ppermute x5, waiting for transfers between devices, swapped(): lax.ppermute(x, axis, [(i, i ^ bit) for i in range(lax.axis_size(axis))])  15.4 us
    all_to_all x3, starting transfers between devices, to_channels(): lax.all_to_all(turned, 'seq', split_axis=0, concat_axis=0, tiled=True)  14.9 us
    all_to_all x2, starting transfers between devices, to_positions(): lax.all_to_all(x.reshape(devices * channels, length), 'seq', split_axis=0...  11.9 us
    dot_general x4, matrix products, on_device(): jnp.dot(pieces[i], w_pieces[i], preferred_element_type=jnp.float32)  9.31 us
    pallas_call x1, Pallas kernels, spectrum(): pl.pallas_call(spectrum_kernel, out_shape=jax.ShapeDtypeStruct((rows, wid...  8.63 us
    dot_general x1, matrix products, on_device(): lax.dot_general(cotangent, w_out, (((1,), (1,)), ((), ())), preferred_ele...  6.92 us
    ppermute x2, starting transfers between devices, passed_along(): return lax.ppermute(x, axis, pairs)  6.13 us
  transfers between devices with their start and end apart: 12, of which 5 were waited for; matrix products, arithmetic and copies ran while one was open for 20% of the time, Pallas kernels for 26%

profile of v3, /device:TPU:0, one launch (start us, length us, event | category | flops | bytes accessed | tf_op | source)
XLA Modules:
  0.0 145.8 jit_solution(9030941859121032309)
XLA Ops:
  0.6 0.8 slice.49
  1.4 4.8 %collective-permute-start = (bf16[3,2,512]{2,1,0:T(2,128)(2,1)S(1)}, bf16[3,2,512]{2,1,0:T(2,128)(2,1)S(1)}, u32[]{:S(2)}, u32[]{:S(2)}) collective-permute-start(bf16[3,2,512]{2,1,0:T(2,128)(2,1)S(1)} %slice.49), channel_id=1, source_target_pairs={{0,4},{4,8},{8,12},{12,16},{16,20},{20,24},{24,28},{1,5},{5,9},{9,... | collective-permute-start | bytes 18440 | tf_op jit(solution)/shard_map/ppermute | solution.py:17
  6.2 1.3 convert_bitcast_fusion
  7.5 1.0 copy.17
  8.5 4.9 %all-to-all-start.1 = ((bf16[8,64,512]{2,1,0:T(8,128)(2,1)}), bf16[8,64,512]{2,1,0:T(8,128)(2,1)}, u32[]{:S(2)}, u32[]{:S(2)}) async-start(bf16[8,64,512]{2,1,0:T(8,128)(2,1)} %bitcast.7), calls=%async_computation.1 | async-start | bytes 1048576 | tf_op jit(solution)/shard_map/all_to_all | solution.py:228
  13.5 0.0 copy-start.4
  13.5 6.9 %fusion.12 = f32[512,512]{1,0:T(8,128)} fusion(bf16[512,4096]{1,0:T(8,128)(2,1)} %param.14, bf16[512,4096]{1,0:T(8,128)(2,1)} %param.13), kind=kOutput, calls=%fused_computation.43 | convolution fusion | flops 2147483648 | bytes 9437184 | tf_op jit(solution)/shard_map/dot_general | solution.py:257
  20.4 0.0 collective-permute-done
  20.4 0.5 maximum_convert_fusion
  20.9 0.9 fusion.3
  21.9 0.3 copy-done.1
  22.1 1.4 convert_bitcast_fusion.1
  23.5 2.1 %copy.16 = bf16[512,512]{1,0:T(8,128)(2,1)} copy(bf16[512,512]{0,1:T(8,128)(2,1)} %get-tuple-element.38) | data formatting | bytes 1048576 | tf_op jit(solution)/shard_map/transpose | solution.py:233
  25.6 2.2 %all-to-all-done.1.x_ref = bf16[8,64,512]{2,1,0:T(8,128)(2,1)} async-done(((bf16[8,64,512]{2,1,0:T(8,128)(2,1)}), bf16[8,64,512]{2,1,0:T(8,128)(2,1)}, u32[]{:S(2)}, u32[]{:S(2)}) %all-to-all-start.1) | async-done | bytes 524320 | tf_op jit(solution)/shard_map/all_to_all | solution.py:228
  27.8 4.2 %all-to-all-start = ((bf16[8,64,512]{2,1,0:T(8,128)(2,1)}), bf16[8,64,512]{2,1,0:T(8,128)(2,1)}, u32[]{:S(2)}, u32[]{:S(2)}) async-start(bf16[8,64,512]{2,1,0:T(8,128)(2,1)} %bitcast.93), calls=%async_computation | async-start | bytes 1048576 | tf_op jit(solution)/shard_map/all_to_all | solution.py:228
  32.0 4.3 %constant_dynamic-slice_fusion = (bf16[512,1024]{1,0:T(8,128)(2,1)}, bf16[512,1024]{1,0:T(8,128)(2,1)}, bf16[512,1024]{1,0:T(8,128)(2,1)}, bf16[512,1024]{1,0:T(8,128)(2,1)}) fusion(bf16[512,4096]{1,0:T(8,128)(2,1)} %param.13, s32[]{:T(128)S(6)} %select_n.15, s32[]{:T(128)S(6)} %select_n.13, s32[]{:T(128)S(6)} %select_n.12, s32[]{:T(128)S(6)} %select_n.14), kind=kLoop, calls=%fused_computation.38 | loop fusion | bytes 8388624 | tf_op jit(solution)/shard_map/dynamic_slice | solution.py:266
  36.2 1.5 %collective-permute-start.1 = (bf16[512,1024]{1,0:T(8,128)(2,1)}, bf16[512,1024]{1,0:T(8,128)(2,1)}, u32[]{:S(2)}, u32[]{:S(2)}) collective-permute-start(bf16[512,1024]{1,0:T(8,128)(2,1)} %get-tuple-element.35), channel_id=1, source_target_pairs={{0,2},{1,3},{2,0},{3,1},{4,6},{5,7},{6,4},{7,5},{8,10},{9,11},{10,... | collective-permute-start | bytes 3145736 | tf_op jit(solution)/shard_map/ppermute | solution.py:223
  37.7 8.6 %shard_map.104.spectrum_hbm = f32[512,1024]{1,0:T(8,128)} custom-call(bf16[8,64,512]{2,1,0:T(8,128)(2,1)} %all-to-all-done.1.x_ref, f32[2,8,512]{2,1,0:T(8,128)} %constant.22.clone.twiddle_ref, bf16[1024,1024]{1,0:T(8,128)(2,1)} %constant.23.clone.table_high, bf16[1024,1024]{1,0:T(8,128)(2,1)} %constant.24.clone.table_low), custom_call_target="tpu_custom_call" | custom-call | flops 3221225472 | bytes 8388608 | tf_op jit(solution)/shard_map/pallas_call | solution.py:192
  46.4 2.0 %copy.18 = bf16[512,512]{1,0:T(8,128)(2,1)} copy(bf16[512,512]{0,1:T(8,128)(2,1)} %get-tuple-element.18) | data formatting | bytes 1048576 | tf_op jit(solution)/shard_map/optimization_barrier | solution.py:269
  48.4 0.0 all-to-all-done.x_ref
  48.4 5.9 %all-to-all-start.2 = ((bf16[8,64,512]{2,1,0:T(8,128)(2,1)}), bf16[8,64,512]{2,1,0:T(8,128)(2,1)}, u32[]{:S(2)}, u32[]{:S(2)}) async-start(bf16[8,64,512]{2,1,0:T(8,128)(2,1)} %bitcast.94), calls=%async_computation.2 | async-start | bytes 1048576 | tf_op jit(solution)/shard_map/all_to_all | solution.py:228
  54.3 0.0 collective-permute-start.3
  54.3 0.6 collective-permute-start.2
  54.9 7.7 %collective-permute-done.1 = bf16[512,1024]{1,0:T(8,128)(2,1)} collective-permute-done((bf16[512,1024]{1,0:T(8,128)(2,1)}, bf16[512,1024]{1,0:T(8,128)(2,1)}, u32[]{:S(2)}, u32[]{:S(2)}) %collective-permute-start.1) | collective-permute-done | bytes 1048608 | tf_op jit(solution)/shard_map/ppermute | solution.py:223
  62.6 14.7 %shard_map.105 = bf16[8,64,512]{2,1,0:T(8,128)(2,1)} custom-call(bf16[8,64,512]{2,1,0:T(8,128)(2,1)} %all-to-all-done.x_ref, f32[2,8,512]{2,1,0:T(8,128)} %constant.22.clone.twiddle_ref, bf16[1024,1024]{1,0:T(8,128)(2,1)} %constant.23.clone.table_high, bf16[1024,1024]{1,0:T(8,128)(2,1)} %constant.24.clone.table_low, f32[512,1024]{1,0:T(8,128)} %shard_map.104.spectrum_hbm), custom_call_target="tpu_custom_call" | custom-call | flops 6442450944 | bytes 8388608 | tf_op jit(solution)/shard_map/pallas_call | solution.py:208
  77.3 5.9 %all-to-all-start.3 = ((bf16[8,64,512]{2,1,0:T(8,128)(2,1)}), bf16[8,64,512]{2,1,0:T(8,128)(2,1)}, u32[]{:S(2)}, u32[]{:S(2)}) async-start(bf16[8,64,512]{2,1,0:T(8,128)(2,1)} %shard_map.105), calls=%async_computation.3 | async-start | bytes 1048576 | tf_op jit(solution)/shard_map/all_to_all | solution.py:238
  83.2 14.7 %shard_map.106 = bf16[8,64,512]{2,1,0:T(8,128)(2,1)} custom-call(bf16[8,64,512]{2,1,0:T(8,128)(2,1)} %all-to-all-done.2.x_ref, f32[2,8,512]{2,1,0:T(8,128)} %constant.22.clone.twiddle_ref, bf16[1024,1024]{1,0:T(8,128)(2,1)} %constant.23.clone.table_high, bf16[1024,1024]{1,0:T(8,128)(2,1)} %constant.24.clone.table_low, f32[512,1024]{1,0:T(8,128)} %shard_map.104.spectrum_hbm), custom_call_target="tpu_custom_call" | custom-call | flops 6442450944 | bytes 8388608 | tf_op jit(solution)/shard_map/pallas_call | solution.py:208
  97.9 0.0 collective-permute-done.3
  97.9 0.0 all-to-all-done.3
  97.9 2.0 %copy.19 = bf16[512,512]{0,1:T(8,128)(2,1)} copy(bf16[512,512]{1,0:T(8,128)(2,1)} %bitcast.9) | data formatting | bytes 1048576 | tf_op jit(solution)/shard_map/optimization_barrier | solution.py:277
  100.0 1.5 %multiply_convert_fusion = bf16[512,512]{1,0:T(8,128)(2,1)S(1)} fusion(f32[3,512,512]{2,1,0:T(8,128)S(1)} %fusion.3, bf16[512,512]{0,1:T(8,128)(2,1)} %copy.19, f32[512]{0:T(512)S(1)} %copy-done.6), kind=kLoop, calls=%fused_computation.23 | loop fusion | flops 1572864 | bytes 4196352 | tf_op jit(solution)/shard_map/convert_element_type | solution.py:281
  101.5 1.6 %collective-permute-start.4 = (bf16[1,512,512]{2,1,0:T(8,128)(2,1)S(1)}, bf16[1,512,512]{2,1,0:T(8,128)(2,1)S(1)}, u32[]{:S(2)}, u32[]{:S(2)}) collective-permute-start(bf16[1,512,512]{2,1,0:T(8,128)(2,1)S(1)} %bitcast.91), channel_id=1, source_target_pairs={{0,2},{1,3},{2,0},{3,1},{4,6},{5,7},{6,4},{7,5},{8,10},{9,11},{10,... | collective-permute-start | bytes 1572872 | tf_op jit(solution)/shard_map/ppermute | solution.py:223
  103.1 7.7 %collective-permute-done.4 = bf16[1,512,512]{2,1,0:T(8,128)(2,1)S(1)} collective-permute-done((bf16[1,512,512]{2,1,0:T(8,128)(2,1)S(1)}, bf16[1,512,512]{2,1,0:T(8,128)(2,1)S(1)}, u32[]{:S(2)}, u32[]{:S(2)}) %collective-permute-start.4) | collective-permute-done | bytes 524320 | tf_op jit(solution)/shard_map/ppermute | solution.py:223
  110.7 1.1 pad_maximum_fusion.2
  111.9 6.0 %all-to-all-start.4 = ((bf16[8,64,512]{2,1,0:T(8,128)(2,1)}), bf16[8,64,512]{2,1,0:T(8,128)(2,1)}, u32[]{:S(2)}, u32[]{:S(2)}) async-start(bf16[8,64,512]{2,1,0:T(8,128)(2,1)} %shard_map.106), calls=%async_computation.4 | async-start | bytes 1048576 | tf_op jit(solution)/shard_map/all_to_all | solution.py:238
  117.9 2.2 %fusion.13 = f32[512,1024]{1,0:T(8,128)S(1)} fusion(bf16[512,512]{1,0:T(8,128)(2,1)} %copy-done, bf16[512,1024]{1,0:T(8,128)(2,1)} %get-tuple-element.24), kind=kOutput, calls=%fused_computation.44 | convolution fusion | flops 536870912 | bytes 3670016 | tf_op jit(solution)/shard_map/dot_general | solution.py:290
  120.0 1.9 %fusion.9 = f32[512,1024]{1,0:T(8,128)S(1)} fusion(bf16[512,1024]{1,0:T(8,128)(2,1)} %collective-permute-done.1, bf16[1,512,512]{2,1,0:T(8,128)(2,1)S(1)} %copy-done.3), kind=kOutput, calls=%fused_computation.30 | convolution fusion | flops 536870912 | bytes 3670016 | tf_op jit(solution)/shard_map/dot_general | solution.py:290
  122.0 0.0 collective-permute-done.5
  122.0 2.1 %fusion.8 = f32[512,1024]{1,0:T(8,128)S(1)} fusion(bf16[512,1024]{1,0:T(8,128)(2,1)} %collective-permute-done.2, bf16[2,512,512]{2,1,0:T(8,128)(2,1)} %collective-permute-done.5), kind=kOutput, calls=%fused_computation.29 | convolution fusion | flops 536870912 | bytes 3670016 | tf_op jit(solution)/shard_map/dot_general | solution.py:290
  124.1 3.1 %add_convert_fusion = bf16[512,1024]{1,0:T(8,128)(2,1)} fusion(f32[512,1024]{1,0:T(8,128)S(1)} %fusion.9, f32[512,1024]{1,0:T(8,128)S(1)} %fusion.13, f32[512,1024]{1,0:T(8,128)S(1)} %fusion.8, bf16[512,1024]{1,0:T(8,128)(2,1)} %collective-permute-done.3, bf16[2,512,512]{2,1,0:T(8,128)(2,1)} %collective-permute-done.5), kind=kOutput, calls=%fused_computation.12 | convolution fusion | flops 538968064 | bytes 8912896 | tf_op jit(solution)/shard_map/dot_general | solution.py:290
  127.2 5.9 %all-to-all-done.4 = bf16[8,64,512]{2,1,0:T(8,128)(2,1)} async-done(((bf16[8,64,512]{2,1,0:T(8,128)(2,1)}), bf16[8,64,512]{2,1,0:T(8,128)(2,1)}, u32[]{:S(2)}, u32[]{:S(2)}) %all-to-all-start.4) | async-done | bytes 524320 | tf_op jit(solution)/shard_map/all_to_all | solution.py:238
  133.1 2.0 %copy.20 = bf16[512,512]{0,1:T(8,128)(2,1)} copy(bf16[512,512]{1,0:T(8,128)(2,1)} %bitcast.10) | data formatting | bytes 1048576 | tf_op jit(solution)/shard_map/optimization_barrier | solution.py:294
  135.2 2.1 %multiply_bitcast_fusion.1 = (f32[1,512,512]{2,1,0:T(8,128)S(1)}, f32[1,512,512]{2,1,0:T(8,128)S(1)}, f32[1,512,512]{2,1,0:T(8,128)S(1)}) fusion(f32[3,512,512]{2,1,0:T(8,128)S(1)} %fusion.3, bf16[512,512]{0,1:T(8,128)(2,1)} %copy.20, f32[512]{0:T(512)S(1)} %copy-done.6, f32[512,512]{1,0:T(8,128)} %fusion.12, bf16[512,512]{0,1:T(8,128)(2,1)} %copy.19), kind=kLoop, calls=%fused_computation.21 | loop fusion | flops 2883584 | bytes 8390656 | tf_op jit(solution)/shard_map/stack | solution.py:296
  137.3 0.3 pad_maximum_fusion.1
  137.6 1.3 collective-permute-start.6
  138.9 4.3 %collective-permute-done.6 = f32[3,2,512]{2,1,0:T(2,128)S(1)} collective-permute-done((f32[3,2,512]{2,1,0:T(2,128)S(1)}, f32[3,2,512]{2,1,0:T(2,128)S(1)}, u32[]{:S(2)}, u32[]{:S(2)}) %collective-permute-start.6) | collective-permute-done | bytes 12320 | tf_op jit(solution)/shard_map/ppermute | solution.py:17
  143.2 0.4 pad_maximum_fusion
  143.6 2.2 %fusion.1 = bf16[3,512,512]{2,1,0:T(8,128)(2,1)} fusion(f32[3,514,512]{2,1,0:T(8,128)S(1)} %pad_maximum_fusion, f32[3,512]{1,0:T(4,128)S(1)} %get-tuple-element.42, f32[3,512]{1,0:T(4,128)S(1)} %get-tuple-element.43, f32[3,512]{1,0:T(4,128)S(1)} %bitcast.96, f32[1,512,512]{2,1,0:T(8,128)S(1)} %get-tuple-element.31, f32[1,512,512]{2,1,0:T(8,128)S(1)} %get-tuple-element.30, ...), kind=kLoop, calls=%fused_computation.3 | loop fusion | flops 6291456 | bytes 11028480 | tf_op jit(solution)/shard_map/convert_element_type | solution.py:304
  (19 shorter events, 0.1 us)
Async XLA Ops:
  0.6 12.8 %copy-start.5 = (f32[3,3,512]{2,1,0:T(4,128)S(1)}, f32[3,3,512]{2,1,0:T(4,128)}, u32[]{:S(2)}) copy-start(f32[3,3,512]{2,1,0:T(4,128)} %param.10) | copy-start | bytes 55300
  1.4 19.0 %collective-permute-start = (bf16[3,2,512]{2,1,0:T(2,128)(2,1)S(1)}, bf16[3,2,512]{2,1,0:T(2,128)(2,1)S(1)}, u32[]{:S(2)}, u32[]{:S(2)}) collective-permute-start(bf16[3,2,512]{2,1,0:T(2,128)(2,1)S(1)} %slice.49), channel_id=1, source_target_pairs={{0,4},{4,8},{8,12},{12,16},{16,20},{20,24},{24,28},{1,5},{5,9},{9,... | collective-permute-start | bytes 18440 | tf_op jit(solution)/shard_map/ppermute | solution.py:17
  8.5 19.2 %all-to-all-start.1 = ((bf16[8,64,512]{2,1,0:T(8,128)(2,1)}), bf16[8,64,512]{2,1,0:T(8,128)(2,1)}, u32[]{:S(2)}, u32[]{:S(2)}) async-start(bf16[8,64,512]{2,1,0:T(8,128)(2,1)} %bitcast.7), calls=%async_computation.1 | async-start | bytes 1048576 | tf_op jit(solution)/shard_map/all_to_all | solution.py:228
  13.5 7.0 %copy-start.4 = (bf16[3,512,512]{2,1,0:T(8,128)(2,1)S(1)}, bf16[3,512,512]{2,1,0:T(8,128)(2,1)}, u32[]{:S(2)}) copy-start(bf16[3,512,512]{2,1,0:T(8,128)(2,1)} %param.9) | copy-start | bytes 4718596
  20.9 1.2 copy-start.1
  27.8 20.6 %all-to-all-start = ((bf16[8,64,512]{2,1,0:T(8,128)(2,1)}), bf16[8,64,512]{2,1,0:T(8,128)(2,1)}, u32[]{:S(2)}, u32[]{:S(2)}) async-start(bf16[8,64,512]{2,1,0:T(8,128)(2,1)} %bitcast.93), calls=%async_computation | async-start | bytes 1048576 | tf_op jit(solution)/shard_map/all_to_all | solution.py:228
  36.2 26.4 %collective-permute-start.1 = (bf16[512,1024]{1,0:T(8,128)(2,1)}, bf16[512,1024]{1,0:T(8,128)(2,1)}, u32[]{:S(2)}, u32[]{:S(2)}) collective-permute-start(bf16[512,1024]{1,0:T(8,128)(2,1)} %get-tuple-element.35), channel_id=1, source_target_pairs={{0,2},{1,3},{2,0},{3,1},{4,6},{5,7},{6,4},{7,5},{8,10},{9,11},{10,... | collective-permute-start | bytes 3145736 | tf_op jit(solution)/shard_map/ppermute | solution.py:223
  48.4 28.9 %all-to-all-start.2 = ((bf16[8,64,512]{2,1,0:T(8,128)(2,1)}), bf16[8,64,512]{2,1,0:T(8,128)(2,1)}, u32[]{:S(2)}, u32[]{:S(2)}) async-start(bf16[8,64,512]{2,1,0:T(8,128)(2,1)} %bitcast.94), calls=%async_computation.2 | async-start | bytes 1048576 | tf_op jit(solution)/shard_map/all_to_all | solution.py:228
  54.3 43.6 %collective-permute-start.3 = (bf16[512,1024]{1,0:T(8,128)(2,1)}, bf16[512,1024]{1,0:T(8,128)(2,1)}, u32[]{:S(2)}, u32[]{:S(2)}) collective-permute-start(bf16[512,1024]{1,0:T(8,128)(2,1)} %get-tuple-element.33), channel_id=1, source_target_pairs={{0,3},{1,2},{2,1},{3,0},{4,7},{5,6},{6,5},{7,4},{8,11},{9,10},{10,... | collective-permute-start | bytes 3145736 | tf_op jit(solution)/shard_map/ppermute | solution.py:223
  54.3 43.6 %collective-permute-start.2 = (bf16[512,1024]{1,0:T(8,128)(2,1)}, bf16[512,1024]{1,0:T(8,128)(2,1)}, u32[]{:S(2)}, u32[]{:S(2)}) collective-permute-start(bf16[512,1024]{1,0:T(8,128)(2,1)} %get-tuple-element.36), channel_id=1, source_target_pairs={{0,1},{1,0},{2,3},{3,2},{4,5},{5,4},{6,7},{7,6},{8,9},{9,8},{10,11... | collective-permute-start | bytes 3145736 | tf_op jit(solution)/shard_map/ppermute | solution.py:223
  77.3 20.6 %all-to-all-start.3 = ((bf16[8,64,512]{2,1,0:T(8,128)(2,1)}), bf16[8,64,512]{2,1,0:T(8,128)(2,1)}, u32[]{:S(2)}, u32[]{:S(2)}) async-start(bf16[8,64,512]{2,1,0:T(8,128)(2,1)} %shard_map.105), calls=%async_computation.3 | async-start | bytes 1048576 | tf_op jit(solution)/shard_map/all_to_all | solution.py:238
  83.2 16.7 %copy-start.6 = (f32[512]{0:T(512)S(1)}, f32[512]{0:T(512)}, u32[]{:S(2)}) copy-start(f32[512]{0:T(512)} %param.12) | copy-start | bytes 6148
  101.4 9.3 %copy-start = (bf16[512,512]{1,0:T(8,128)(2,1)}, bf16[512,512]{1,0:T(8,128)(2,1)S(1)}, u32[]{:S(2)}) copy-start(bf16[512,512]{1,0:T(8,128)(2,1)S(1)} %multiply_convert_fusion) | copy-start | bytes 1572868
  101.5 9.3 %collective-permute-start.4 = (bf16[1,512,512]{2,1,0:T(8,128)(2,1)S(1)}, bf16[1,512,512]{2,1,0:T(8,128)(2,1)S(1)}, u32[]{:S(2)}, u32[]{:S(2)}) collective-permute-start(bf16[1,512,512]{2,1,0:T(8,128)(2,1)S(1)} %bitcast.91), channel_id=1, source_target_pairs={{0,2},{1,3},{2,0},{3,1},{4,6},{5,7},{6,4},{7,5},{8,10},{9,11},{10,... | collective-permute-start | bytes 1572872 | tf_op jit(solution)/shard_map/ppermute | solution.py:223
  110.7 1.1 copy-start.2
  111.9 10.1 %collective-permute-start.5 = (bf16[2,512,512]{2,1,0:T(8,128)(2,1)}, bf16[2,512,512]{2,1,0:T(8,128)(2,1)}, u32[]{:S(2)}, u32[]{:S(2)}) collective-permute-start(bf16[2,512,512]{2,1,0:T(8,128)(2,1)} %pad_maximum_fusion.2), channel_id=1, source_target_pairs={{0,1},{1,0},{2,3},{3,2},{4,5},{5,4},{6,7},{7,6},{8,9},{9,8},{10,11... | collective-permute-start | bytes 3145736 | tf_op jit(solution)/shard_map/ppermute | solution.py:223
  111.9 21.2 %all-to-all-start.4 = ((bf16[8,64,512]{2,1,0:T(8,128)(2,1)}), bf16[8,64,512]{2,1,0:T(8,128)(2,1)}, u32[]{:S(2)}, u32[]{:S(2)}) async-start(bf16[8,64,512]{2,1,0:T(8,128)(2,1)} %shard_map.106), calls=%async_computation.4 | async-start | bytes 1048576 | tf_op jit(solution)/shard_map/all_to_all | solution.py:238
  117.9 2.2 %copy-start.3 = (bf16[1,512,512]{2,1,0:T(8,128)(2,1)S(1)}, bf16[1,512,512]{2,1,0:T(8,128)(2,1)}, u32[]{:S(2)}) copy-start(bf16[1,512,512]{2,1,0:T(8,128)(2,1)} %copy-done.2) | copy-start | bytes 1572868
  137.6 5.6 %collective-permute-start.6 = (f32[3,2,512]{2,1,0:T(2,128)S(1)}, f32[3,2,512]{2,1,0:T(2,128)S(1)}, u32[]{:S(2)}, u32[]{:S(2)}) collective-permute-start(f32[3,2,512]{2,1,0:T(2,128)S(1)} %slice.71), channel_id=1, source_target_pairs={{4,0},{8,4},{12,8},{16,12},{20,16},{24,20},{28,24},{5,1},{9,5},{13... | collective-permute-start | bytes 36872 | tf_op jit(solution)/shard_map/ppermute | solution.py:17

commit v4 on v3

--- a/solution.py
+++ b/solution.py
@@ -268,11 +268,11 @@
     taps_spectrum = spectrum(taps_channels, tables)
     grad_turned, taps_spectrum = lax.optimization_barrier((turned_over(grad_state), taps_spectrum))
     early = 2 % shares
-    source_channels, w_pieces[early] = lax.optimization_barrier(
-        (to_channels(turned_over(source)), w_pieces[early])
-    )
+    source_channels = to_channels(turned_over(source))
     state_channels = filtered(source_channels, taps_spectrum, tables, 1.0)
-    state_channels, grad_received = lax.optimization_barrier((state_channels, to_channels(grad_turned)))
+    state_channels, grad_received, w_pieces[early] = lax.optimization_barrier(
+        (state_channels, to_channels(grad_turned), w_pieces[early])
+    )
     grad_channels = filtered(grad_received, taps_spectrum, tables, -1.0)
     state_positions, grad_channels, w_pieces = lax.optimization_barrier(
         (to_positions(state_channels), grad_channels, w_pieces)
@@ -283,6 +283,8 @@
     bit = shares // 2
     while bit:
         order = sorted(pieces)
+        if bit == 1:
+            grad_positions, pieces = lax.optimization_barrier((to_positions(grad_channels), pieces))
         received = swapped(jnp.stack([pieces[i] for i in order]), "tp", bit)
         pieces.update({i ^ bit: received[at] for at, i in enumerate(order)})
         bit //= 2
@@ -291,7 +293,6 @@
     )
     mixed = total.astype(jnp.bfloat16)
     grad_q = grad_gated * mixer_state
-    grad_positions, mixed = lax.optimization_barrier((to_positions(grad_channels), mixed))
     grad_source = grad_positions.T.astype(jnp.float32) + skip_gain * grad_state
     gradients = jnp.stack([grad_q, grad_source * conv_v, grad_source * conv_k])
     following = passed_along(gradients[:, :2, :], "seq", -1)

time: 147 us -> 135 us (0.918)
  waiting for transfers between devices: 27.8 us -> 17.3 us
  matrix products: 16.2 us -> 13.8 us
    all_to_all x2, waiting for transfers between devices: 5.92 us -> 0.07 us  [to_positions(): lax.all_to_all(x.reshape(devices * channels, length), 'seq', split_axis=0...]
    ppermute x5, waiting for transfers between devices: 15.4 us -> 11.6 us  [swapped(): lax.ppermute(x, axis, [(i, i ^ bit) for i in range(lax.axis_size(axis))])]
    ppermute x2, waiting for transfers between devices: 4.29 us -> 2.19 us  [passed_along(): return lax.ppermute(x, axis, pairs)]
  transfers between devices with their start and end apart: 12 -> 12, of which waited for: 5 -> 4; matrix products, arithmetic and copies ran while one was open for 20% -> 21% of each run, Pallas kernels for 26% -> 28%
where the time goes in v4:
time: 135 us; the launch traced here: 134 us
  Pallas kernels  37.9 us (28%)
  starting transfers between devices  36.7 us (27%)
  waiting for transfers between devices  17.3 us (13%)
  local copies, waits for them, and re-layouts  15.1 us (11%)
  matrix products  13.8 us (10%)
  other arithmetic  11.8 us (9%)
    pallas_call x2, Pallas kernels, filtered(): pl.pallas_call(functools.partial(filter_kernel, sign), out_shape=jax.Shap...  29.3 us
    all_to_all x3, starting transfers between devices, to_channels(): lax.all_to_all(turned, 'seq', split_axis=0, concat_axis=0, tiled=True)  14.9 us
    all_to_all x2, starting transfers between devices, to_positions(): lax.all_to_all(x.reshape(devices * channels, length), 'seq', split_axis=0...  12 us
    ppermute x5, waiting for transfers between devices, swapped(): lax.ppermute(x, axis, [(i, i ^ bit) for i in range(lax.axis_size(axis))])  11.6 us
    pallas_call x1, Pallas kernels, spectrum(): pl.pallas_call(spectrum_kernel, out_shape=jax.ShapeDtypeStruct((rows, wid...  8.63 us
    dot_general x4, matrix products, on_device(): jnp.dot(pieces[i], w_pieces[i], preferred_element_type=jnp.float32)  7.86 us
    ppermute x2, starting transfers between devices, passed_along(): return lax.ppermute(x, axis, pairs)  6.13 us
    dot_general x1, matrix products, on_device(): lax.dot_general(cotangent, w_out, (((1,), (1,)), ((), ())), preferred_ele...  5.93 us
  transfers between devices with their start and end apart: 12, of which 4 were waited for; matrix products, arithmetic and copies ran while one was open for 21% of the time, Pallas kernels for 28%

profile of v4, /device:TPU:0, one launch (start us, length us, event | category | flops | bytes accessed | tf_op | source)
XLA Modules:
  0.0 133.6 jit_solution(15779110686241836329)
XLA Ops:
  0.6 0.8 slice.49
  1.4 4.8 %collective-permute-start = (bf16[3,2,512]{2,1,0:T(2,128)(2,1)S(1)}, bf16[3,2,512]{2,1,0:T(2,128)(2,1)S(1)}, u32[]{:S(2)}, u32[]{:S(2)}) collective-permute-start(bf16[3,2,512]{2,1,0:T(2,128)(2,1)S(1)} %slice.49), channel_id=1, source_target_pairs={{0,4},{4,8},{8,12},{12,16},{16,20},{20,24},{24,28},{1,5},{5,9},{9,... | collective-permute-start | bytes 18440 | tf_op jit(solution)/shard_map/ppermute | solution.py:17
  6.2 1.3 convert_bitcast_fusion
  7.5 1.0 copy.17
  8.5 4.9 %all-to-all-start.1 = ((bf16[8,64,512]{2,1,0:T(8,128)(2,1)}), bf16[8,64,512]{2,1,0:T(8,128)(2,1)}, u32[]{:S(2)}, u32[]{:S(2)}) async-start(bf16[8,64,512]{2,1,0:T(8,128)(2,1)} %bitcast.7), calls=%async_computation.1 | async-start | bytes 1048576 | tf_op jit(solution)/shard_map/all_to_all | solution.py:228
  13.5 0.0 copy-start.4
  13.5 5.9 %fusion.10 = f32[512,512]{1,0:T(8,128)S(1)} fusion(bf16[512,4096]{1,0:T(8,128)(2,1)} %param.14, bf16[512,4096]{1,0:T(8,128)(2,1)} %param.13), kind=kOutput, calls=%fused_computation.41 | convolution fusion | flops 2147483648 | bytes 9437184 | tf_op jit(solution)/shard_map/dot_general | solution.py:257
  19.4 0.0 collective-permute-done
  19.5 0.5 maximum_convert_fusion
  19.9 0.9 fusion.3
  20.9 1.4 %convert_bitcast_fusion.1 = (bf16[512,512]{0,1:T(8,128)(2,1)}, bf16[512,512]{0,1:T(8,128)(2,1)}) fusion(f32[512,512]{1,0:T(8,128)S(1)} %fusion.10, f32[3,512,512]{2,1,0:T(8,128)S(1)} %fusion.3), kind=kLoop, calls=%fused_computation.31 | loop fusion | flops 1048576 | bytes 5242880 | tf_op jit(solution)/shard_map/transpose | solution.py:233
  22.2 2.1 %copy.16 = bf16[512,512]{1,0:T(8,128)(2,1)} copy(bf16[512,512]{0,1:T(8,128)(2,1)} %get-tuple-element.38) | data formatting | bytes 1048576 | tf_op jit(solution)/shard_map/transpose | solution.py:233
  24.3 3.5 %all-to-all-done.1.x_ref = bf16[8,64,512]{2,1,0:T(8,128)(2,1)} async-done(((bf16[8,64,512]{2,1,0:T(8,128)(2,1)}), bf16[8,64,512]{2,1,0:T(8,128)(2,1)}, u32[]{:S(2)}, u32[]{:S(2)}) %all-to-all-start.1) | async-done | bytes 524320 | tf_op jit(solution)/shard_map/all_to_all | solution.py:228
  27.8 4.2 %all-to-all-start = ((bf16[8,64,512]{2,1,0:T(8,128)(2,1)}), bf16[8,64,512]{2,1,0:T(8,128)(2,1)}, u32[]{:S(2)}, u32[]{:S(2)}) async-start(bf16[8,64,512]{2,1,0:T(8,128)(2,1)} %bitcast.94), calls=%async_computation | async-start | bytes 1048576 | tf_op jit(solution)/shard_map/all_to_all | solution.py:228
  32.0 4.3 %constant_dynamic-slice_fusion = (bf16[512,1024]{1,0:T(8,128)(2,1)}, bf16[512,1024]{1,0:T(8,128)(2,1)}, bf16[512,1024]{1,0:T(8,128)(2,1)}, bf16[512,1024]{1,0:T(8,128)(2,1)}) fusion(bf16[512,4096]{1,0:T(8,128)(2,1)} %param.13, s32[]{:T(128)S(6)} %select_n.15, s32[]{:T(128)S(6)} %select_n.13, s32[]{:T(128)S(6)} %select_n.12, s32[]{:T(128)S(6)} %select_n.14), kind=kLoop, calls=%fused_computation.36 | loop fusion | bytes 8388624 | tf_op jit(solution)/shard_map/dynamic_slice | solution.py:266
  36.2 1.5 %collective-permute-start.1 = (bf16[512,1024]{1,0:T(8,128)(2,1)}, bf16[512,1024]{1,0:T(8,128)(2,1)}, u32[]{:S(2)}, u32[]{:S(2)}) collective-permute-start(bf16[512,1024]{1,0:T(8,128)(2,1)} %get-tuple-element.35), channel_id=1, source_target_pairs={{0,2},{1,3},{2,0},{3,1},{4,6},{5,7},{6,4},{7,5},{8,10},{9,11},{10,... | collective-permute-start | bytes 3145736 | tf_op jit(solution)/shard_map/ppermute | solution.py:223
  37.8 8.6 %shard_map.104.spectrum_hbm = f32[512,1024]{1,0:T(8,128)} custom-call(bf16[8,64,512]{2,1,0:T(8,128)(2,1)} %all-to-all-done.1.x_ref, f32[2,8,512]{2,1,0:T(8,128)} %constant.22.clone.twiddle_ref, bf16[1024,1024]{1,0:T(8,128)(2,1)} %constant.23.clone.table_high, bf16[1024,1024]{1,0:T(8,128)(2,1)} %constant.24.clone.table_low), custom_call_target="tpu_custom_call" | custom-call | flops 3221225472 | bytes 8388608 | tf_op jit(solution)/shard_map/pallas_call | solution.py:192
  46.4 2.1 %copy.18 = bf16[512,512]{1,0:T(8,128)(2,1)} copy(bf16[512,512]{0,1:T(8,128)(2,1)} %get-tuple-element.17) | data formatting | bytes 1048576 | tf_op jit(solution)/shard_map/optimization_barrier | solution.py:269
  48.5 0.0 all-to-all-done.x_ref
  48.5 5.9 %all-to-all-start.2 = ((bf16[8,64,512]{2,1,0:T(8,128)(2,1)}), bf16[8,64,512]{2,1,0:T(8,128)(2,1)}, u32[]{:S(2)}, u32[]{:S(2)}) async-start(bf16[8,64,512]{2,1,0:T(8,128)(2,1)} %bitcast.95), calls=%async_computation.2 | async-start | bytes 1048576 | tf_op jit(solution)/shard_map/all_to_all | solution.py:228
  54.3 0.0 collective-permute-start.3
  54.4 0.6 collective-permute-start.2
  55.0 14.6 %shard_map.105 = bf16[8,64,512]{2,1,0:T(8,128)(2,1)} custom-call(bf16[8,64,512]{2,1,0:T(8,128)(2,1)} %all-to-all-done.x_ref, f32[2,8,512]{2,1,0:T(8,128)} %constant.22.clone.twiddle_ref, bf16[1024,1024]{1,0:T(8,128)(2,1)} %constant.23.clone.table_high, bf16[1024,1024]{1,0:T(8,128)(2,1)} %constant.24.clone.table_low, f32[512,1024]{1,0:T(8,128)} %shard_map.104.spectrum_hbm), custom_call_target="tpu_custom_call" | custom-call | flops 6442450944 | bytes 8388608 | tf_op jit(solution)/shard_map/pallas_call | solution.py:208
  69.6 0.0 collective-permute-done.1
  69.6 6.0 %all-to-all-start.3 = ((bf16[8,64,512]{2,1,0:T(8,128)(2,1)}), bf16[8,64,512]{2,1,0:T(8,128)(2,1)}, u32[]{:S(2)}, u32[]{:S(2)}) async-start(bf16[8,64,512]{2,1,0:T(8,128)(2,1)} %shard_map.105), calls=%async_computation.3 | async-start | bytes 1048576 | tf_op jit(solution)/shard_map/all_to_all | solution.py:238
  75.6 14.7 %shard_map.106 = bf16[8,64,512]{2,1,0:T(8,128)(2,1)} custom-call(bf16[8,64,512]{2,1,0:T(8,128)(2,1)} %all-to-all-done.2.x_ref, f32[2,8,512]{2,1,0:T(8,128)} %constant.22.clone.twiddle_ref, bf16[1024,1024]{1,0:T(8,128)(2,1)} %constant.23.clone.table_high, bf16[1024,1024]{1,0:T(8,128)(2,1)} %constant.24.clone.table_low, f32[512,1024]{1,0:T(8,128)} %shard_map.104.spectrum_hbm), custom_call_target="tpu_custom_call" | custom-call | flops 6442450944 | bytes 8388608 | tf_op jit(solution)/shard_map/pallas_call | solution.py:208
  90.3 0.0 collective-permute-done.2
  90.3 0.1 all-to-all-done.3
  90.4 6.0 %all-to-all-start.4 = ((bf16[8,64,512]{2,1,0:T(8,128)(2,1)}), bf16[8,64,512]{2,1,0:T(8,128)(2,1)}, u32[]{:S(2)}, u32[]{:S(2)}) async-start(bf16[8,64,512]{2,1,0:T(8,128)(2,1)} %shard_map.106), calls=%async_computation.4 | async-start | bytes 1048576 | tf_op jit(solution)/shard_map/all_to_all | solution.py:238
  96.3 2.0 %copy.19 = bf16[512,512]{0,1:T(8,128)(2,1)} copy(bf16[512,512]{1,0:T(8,128)(2,1)} %bitcast.9) | data formatting | bytes 1048576 | tf_op jit(solution)/shard_map/optimization_barrier | solution.py:277
  98.4 1.5 %multiply_convert_fusion = bf16[512,512]{1,0:T(8,128)(2,1)S(1)} fusion(f32[3,512,512]{2,1,0:T(8,128)S(1)} %fusion.3, bf16[512,512]{0,1:T(8,128)(2,1)} %copy.19, f32[512]{0:T(512)S(1)} %copy-done.6), kind=kLoop, calls=%fused_computation.23 | loop fusion | flops 1572864 | bytes 4196352 | tf_op jit(solution)/shard_map/convert_element_type | solution.py:281
  99.9 0.8 copy-done
  100.7 1.5 %collective-permute-start.4 = (bf16[1,512,512]{2,1,0:T(8,128)(2,1)S(1)}, bf16[1,512,512]{2,1,0:T(8,128)(2,1)}, u32[]{:S(2)}, u32[]{:S(2)}) collective-permute-start(bf16[1,512,512]{2,1,0:T(8,128)(2,1)S(1)} %bitcast.92), channel_id=1, source_target_pairs={{0,2},{1,3},{2,0},{3,1},{4,6},{5,7},{6,4},{7,5},{8,10},{9,11},{10,... | collective-permute-start | bytes 1572872 | tf_op jit(solution)/shard_map/ppermute | solution.py:223
  102.2 11.6 %collective-permute-done.4 = bf16[1,512,512]{2,1,0:T(8,128)(2,1)} collective-permute-done((bf16[1,512,512]{2,1,0:T(8,128)(2,1)S(1)}, bf16[1,512,512]{2,1,0:T(8,128)(2,1)}, u32[]{:S(2)}, u32[]{:S(2)}) %collective-permute-start.4) | collective-permute-done | bytes 524320 | tf_op jit(solution)/shard_map/ppermute | solution.py:223
  113.7 0.0 all-to-all-done.4
  113.8 2.1 %copy.20 = bf16[512,512]{0,1:T(8,128)(2,1)} copy(bf16[512,512]{1,0:T(8,128)(2,1)} %bitcast.10) | data formatting | bytes 1048576 | tf_op jit(solution)/shard_map/optimization_barrier | solution.py:287
  115.8 2.2 %multiply_bitcast_fusion.1 = (f32[1,512,512]{2,1,0:T(8,128)S(1)}, f32[1,512,512]{2,1,0:T(8,128)S(1)}, f32[1,512,512]{2,1,0:T(8,128)S(1)}) fusion(f32[3,512,512]{2,1,0:T(8,128)S(1)} %fusion.3, bf16[512,512]{0,1:T(8,128)(2,1)} %copy.20, f32[512]{0:T(512)S(1)} %copy-done.6, f32[512,512]{1,0:T(8,128)} %copy-done.2, bf16[512,512]{0,1:T(8,128)(2,1)} %copy.19), kind=kLoop, calls=%fused_computation.21 | loop fusion | flops 2883584 | bytes 8390656 | tf_op jit(solution)/shard_map/stack | solution.py:297
  118.1 0.7 fusion.11
  118.8 1.1 pad_maximum_fusion.2
  120.0 0.1 collective-permute-start.5
  120.0 0.3 pad_maximum_fusion.1
  120.4 1.3 collective-permute-start.6
  121.7 2.1 %fusion.12 = f32[512,1024]{1,0:T(8,128)S(1)} fusion(bf16[512,512]{1,0:T(8,128)(2,1)} %bitcast.13, bf16[512,1024]{1,0:T(8,128)(2,1)} %collective-permute-done.1), kind=kOutput, calls=%fused_computation.43 | convolution fusion | flops 536870912 | bytes 3670016 | tf_op jit(solution)/shard_map/dot_general | solution.py:292
  123.8 2.2 %collective-permute-done.6 = f32[3,2,512]{2,1,0:T(2,128)S(1)} collective-permute-done((f32[3,2,512]{2,1,0:T(2,128)S(1)}, f32[3,2,512]{2,1,0:T(2,128)S(1)}, u32[]{:S(2)}, u32[]{:S(2)}) %collective-permute-start.6) | collective-permute-done | bytes 12320 | tf_op jit(solution)/shard_map/ppermute | solution.py:17
  125.9 0.4 pad_maximum_fusion
  126.4 2.2 %fusion.1 = bf16[3,512,512]{2,1,0:T(8,128)(2,1)} fusion(f32[3,514,512]{2,1,0:T(8,128)S(1)} %pad_maximum_fusion, f32[3,512]{1,0:T(4,128)S(1)} %get-tuple-element.42, f32[3,512]{1,0:T(4,128)S(1)} %get-tuple-element.43, f32[3,512]{1,0:T(4,128)S(1)} %bitcast.97, f32[1,512,512]{2,1,0:T(8,128)S(1)} %get-tuple-element.31, f32[1,512,512]{2,1,0:T(8,128)S(1)} %get-tuple-element.30, ...), kind=kLoop, calls=%fused_computation.3 | loop fusion | flops 6291456 | bytes 11028480 | tf_op jit(solution)/shard_map/convert_element_type | solution.py:305
  128.6 1.9 %fusion.8 = f32[512,1024]{1,0:T(8,128)S(1)} fusion(bf16[512,1024]{1,0:T(8,128)(2,1)} %collective-permute-done.2, bf16[2,512,512]{2,1,0:T(8,128)(2,1)S(1)} %collective-permute-done.5), kind=kOutput, calls=%fused_computation.29 | convolution fusion | flops 536870912 | bytes 3670016 | tf_op jit(solution)/shard_map/dot_general | solution.py:292
  130.5 3.1 %add_convert_fusion = bf16[512,1024]{1,0:T(8,128)(2,1)} fusion(f32[512,1024]{1,0:T(8,128)S(1)} %fusion.12, f32[512,1024]{1,0:T(8,128)S(1)} %fusion.11, f32[512,1024]{1,0:T(8,128)S(1)} %fusion.8, bf16[512,1024]{1,0:T(8,128)(2,1)} %collective-permute-done.3, bf16[2,512,512]{2,1,0:T(8,128)(2,1)S(1)} %collective-permute-done.5), kind=kOutput, calls=%fused_computation.12 | convolution fusion | flops 538968064 | bytes 8912896 | tf_op jit(solution)/shard_map/dot_general | solution.py:292
  (19 shorter events, 0.1 us)
Async XLA Ops:
  0.6 12.8 %copy-start.5 = (f32[3,3,512]{2,1,0:T(4,128)S(1)}, f32[3,3,512]{2,1,0:T(4,128)}, u32[]{:S(2)}) copy-start(f32[3,3,512]{2,1,0:T(4,128)} %param.10) | copy-start | bytes 55300
  1.4 18.0 %collective-permute-start = (bf16[3,2,512]{2,1,0:T(2,128)(2,1)S(1)}, bf16[3,2,512]{2,1,0:T(2,128)(2,1)S(1)}, u32[]{:S(2)}, u32[]{:S(2)}) collective-permute-start(bf16[3,2,512]{2,1,0:T(2,128)(2,1)S(1)} %slice.49), channel_id=1, source_target_pairs={{0,4},{4,8},{8,12},{12,16},{16,20},{20,24},{24,28},{1,5},{5,9},{9,... | collective-permute-start | bytes 18440 | tf_op jit(solution)/shard_map/ppermute | solution.py:17
  8.5 19.2 %all-to-all-start.1 = ((bf16[8,64,512]{2,1,0:T(8,128)(2,1)}), bf16[8,64,512]{2,1,0:T(8,128)(2,1)}, u32[]{:S(2)}, u32[]{:S(2)}) async-start(bf16[8,64,512]{2,1,0:T(8,128)(2,1)} %bitcast.7), calls=%async_computation.1 | async-start | bytes 1048576 | tf_op jit(solution)/shard_map/all_to_all | solution.py:228
  13.5 6.0 %copy-start.4 = (bf16[3,512,512]{2,1,0:T(8,128)(2,1)S(1)}, bf16[3,512,512]{2,1,0:T(8,128)(2,1)}, u32[]{:S(2)}) copy-start(bf16[3,512,512]{2,1,0:T(8,128)(2,1)} %param.9) | copy-start | bytes 4718596
  19.4 1.5 %copy-start.2 = (f32[512,512]{1,0:T(8,128)}, f32[512,512]{1,0:T(8,128)S(1)}, u32[]{:S(2)}) copy-start(f32[512,512]{1,0:T(8,128)S(1)} %fusion.10) | copy-start | bytes 3145732
  27.8 20.7 %all-to-all-start = ((bf16[8,64,512]{2,1,0:T(8,128)(2,1)}), bf16[8,64,512]{2,1,0:T(8,128)(2,1)}, u32[]{:S(2)}, u32[]{:S(2)}) async-start(bf16[8,64,512]{2,1,0:T(8,128)(2,1)} %bitcast.94), calls=%async_computation | async-start | bytes 1048576 | tf_op jit(solution)/shard_map/all_to_all | solution.py:228
  36.2 33.3 %collective-permute-start.1 = (bf16[512,1024]{1,0:T(8,128)(2,1)}, bf16[512,1024]{1,0:T(8,128)(2,1)}, u32[]{:S(2)}, u32[]{:S(2)}) collective-permute-start(bf16[512,1024]{1,0:T(8,128)(2,1)} %get-tuple-element.35), channel_id=1, source_target_pairs={{0,2},{1,3},{2,0},{3,1},{4,6},{5,7},{6,4},{7,5},{8,10},{9,11},{10,... | collective-permute-start | bytes 3145736 | tf_op jit(solution)/shard_map/ppermute | solution.py:223
  48.5 21.1 %all-to-all-start.2 = ((bf16[8,64,512]{2,1,0:T(8,128)(2,1)}), bf16[8,64,512]{2,1,0:T(8,128)(2,1)}, u32[]{:S(2)}, u32[]{:S(2)}) async-start(bf16[8,64,512]{2,1,0:T(8,128)(2,1)} %bitcast.95), calls=%async_computation.2 | async-start | bytes 1048576 | tf_op jit(solution)/shard_map/all_to_all | solution.py:228
  54.3 35.9 %collective-permute-start.3 = (bf16[512,1024]{1,0:T(8,128)(2,1)}, bf16[512,1024]{1,0:T(8,128)(2,1)}, u32[]{:S(2)}, u32[]{:S(2)}) collective-permute-start(bf16[512,1024]{1,0:T(8,128)(2,1)} %get-tuple-element.33), channel_id=1, source_target_pairs={{0,3},{1,2},{2,1},{3,0},{4,7},{5,6},{6,5},{7,4},{8,11},{9,10},{10,... | collective-permute-start | bytes 3145736 | tf_op jit(solution)/shard_map/ppermute | solution.py:223
  54.4 35.9 %collective-permute-start.2 = (bf16[512,1024]{1,0:T(8,128)(2,1)}, bf16[512,1024]{1,0:T(8,128)(2,1)}, u32[]{:S(2)}, u32[]{:S(2)}) collective-permute-start(bf16[512,1024]{1,0:T(8,128)(2,1)} %get-tuple-element.36), channel_id=1, source_target_pairs={{0,1},{1,0},{2,3},{3,2},{4,5},{5,4},{6,7},{7,6},{8,9},{9,8},{10,11... | collective-permute-start | bytes 3145736 | tf_op jit(solution)/shard_map/ppermute | solution.py:223
  69.6 20.8 %all-to-all-start.3 = ((bf16[8,64,512]{2,1,0:T(8,128)(2,1)}), bf16[8,64,512]{2,1,0:T(8,128)(2,1)}, u32[]{:S(2)}, u32[]{:S(2)}) async-start(bf16[8,64,512]{2,1,0:T(8,128)(2,1)} %shard_map.105), calls=%async_computation.3 | async-start | bytes 1048576 | tf_op jit(solution)/shard_map/all_to_all | solution.py:238
  75.6 22.8 %copy-start.6 = (f32[512]{0:T(512)S(1)}, f32[512]{0:T(512)}, u32[]{:S(2)}) copy-start(f32[512]{0:T(512)} %param.12) | copy-start | bytes 6148
  90.4 23.4 %all-to-all-start.4 = ((bf16[8,64,512]{2,1,0:T(8,128)(2,1)}), bf16[8,64,512]{2,1,0:T(8,128)(2,1)}, u32[]{:S(2)}, u32[]{:S(2)}) async-start(bf16[8,64,512]{2,1,0:T(8,128)(2,1)} %shard_map.106), calls=%async_computation.4 | async-start | bytes 1048576 | tf_op jit(solution)/shard_map/all_to_all | solution.py:238
  99.9 0.8 copy-start
  100.7 13.1 %collective-permute-start.4 = (bf16[1,512,512]{2,1,0:T(8,128)(2,1)S(1)}, bf16[1,512,512]{2,1,0:T(8,128)(2,1)}, u32[]{:S(2)}, u32[]{:S(2)}) collective-permute-start(bf16[1,512,512]{2,1,0:T(8,128)(2,1)S(1)} %bitcast.92), channel_id=1, source_target_pairs={{0,2},{1,3},{2,0},{3,1},{4,6},{5,7},{6,4},{7,5},{8,10},{9,11},{10,... | collective-permute-start | bytes 1572872 | tf_op jit(solution)/shard_map/ppermute | solution.py:223
  115.8 2.2 %copy-start.1 = (bf16[512,512]{1,0:T(8,128)(2,1)S(1)}, bf16[512,512]{1,0:T(8,128)(2,1)}, u32[]{:S(2)}) copy-start(bf16[512,512]{1,0:T(8,128)(2,1)} %copy-done) | copy-start | bytes 1572868
  115.8 2.3 %copy-start.3 = (bf16[512,1024]{1,0:T(8,128)(2,1)S(1)}, bf16[512,1024]{1,0:T(8,128)(2,1)}, u32[]{:S(2)}) copy-start(bf16[512,1024]{1,0:T(8,128)(2,1)} %get-tuple-element.24) | copy-start | bytes 3145732
  120.0 8.6 %collective-permute-start.5 = (bf16[2,512,512]{2,1,0:T(8,128)(2,1)S(1)}, bf16[2,512,512]{2,1,0:T(8,128)(2,1)S(1)}, u32[]{:S(2)}, u32[]{:S(2)}) collective-permute-start(bf16[2,512,512]{2,1,0:T(8,128)(2,1)S(1)} %pad_maximum_fusion.2), channel_id=1, source_target_pairs={{0,1},{1,0},{2,3},{3,2},{4,5},{5,4},{6,7},{7,6},{8,9},{9,8},{10,11... | collective-permute-start | bytes 3145736 | tf_op jit(solution)/shard_map/ppermute | solution.py:223
  120.4 5.6 %collective-permute-start.6 = (f32[3,2,512]{2,1,0:T(2,128)S(1)}, f32[3,2,512]{2,1,0:T(2,128)S(1)}, u32[]{:S(2)}, u32[]{:S(2)}) collective-permute-start(f32[3,2,512]{2,1,0:T(2,128)S(1)} %slice.71), channel_id=1, source_target_pairs={{4,0},{8,4},{12,8},{16,12},{20,16},{24,20},{28,24},{5,1},{9,5},{13... | collective-permute-start | bytes 36872 | tf_op jit(solution)/shard_map/ppermute | solution.py:17
